TPU v7x, 768 devices: a whole 4x8x12 slice. The times are simulated.
768 devices in a mesh: fsdp: 96 (over z_lo, x, y), dp: 8 (over z_hi, core).
Axes of the slice: x: 4, y: 8, z: 12 (z_hi: 4, z_lo: 3; z = z_hi * 3 + z_lo), core: 2. Of those that a mesh axis runs over, the one named last changes fastest.
Arguments:
- hidden: bfloat16 [98304, 8192], P(('fsdp', 'dp')), may hold values from -6 to 6
- norm_gain: float32 [8192], replicated, may hold values from 0.1 to 1.9
- proj: bfloat16 [768, 8192], P('fsdp'), may hold values from -2 to 2
- assign: int32 [96, 1024], P('fsdp'), may hold values from 0 to 1023, as said below
- lengths: int32 [8, 4], P('dp'), may hold values from 1 to 6144, 12288 in all within a row
Outputs:
- head_out: bfloat16 [98304, 512], P(('fsdp', 'dp'))
Inputs may be any that keep to these rules, and one draw needn't show every extreme that they name: Each row assign[f] is a permutation of the 1024 indices; of the 128 home rows of one device (entries d * 128 to (d + 1) * 128 - 1), exactly 16 go to each data group g (values g * 128 to g * 128 + 127).
All inputs are finite; a program needn't handle non-finite values.
Results may differ from a plain program's by a relative error of at most 0.02.
The roundings to bfloat16 on the way count: a program that leaves them out, or rounds other values in their place, can miss the bound.
Values may be sent and summed in bfloat16 or wider, within the bound.
No kernel may reach another device: no remote copies, remote signals or barrier semaphores. Data moves between devices by JAX's collectives and lax.ppermute only.
A program may use at most 64 MiB of HBM per device.

v0:
```python
import math

import jax
import jax.numpy as jnp
from jax import lax
from jax.sharding import PartitionSpec as P

QH = 4


THETA = 1000000.0
EPSILON = 1e-06


def from_behind(value, axis, by):
    peers = lax.axis_size(axis)
    pairs = [(i, i + by) for i in range(peers) if 0 <= i + by < peers]
    return lax.ppermute(value, axis, pairs)


def rms_normed(block_rows, norm_gain):
    widened = block_rows.astype(jnp.float32)
    inverse = lax.rsqrt(jnp.mean(widened * widened, axis=1, keepdims=True) + EPSILON)
    return (widened * inverse * norm_gain).astype(jnp.bfloat16)


def rotated(values, positions):
    half_width = values.shape[1] // 2
    inverse_freq = THETA ** (-(jnp.arange(half_width, dtype=jnp.float32) * 2.0) / values.shape[1])
    angles = positions.astype(jnp.float32)[:, None] * inverse_freq[None, :]
    cosine = jnp.cos(angles)
    sine_part = jnp.sin(angles)
    first_half = values[:, :half_width]
    second_half = values[:, half_width:]
    return jnp.concatenate(
        [
            first_half * cosine - second_half * sine_part,
            second_half * cosine + first_half * sine_part,
        ],
        axis=1,
    )


def segment_info(indices, seq_lengths):
    ends_at = jnp.cumsum(seq_lengths)
    finished = ends_at[None, :] <= indices[:, None]
    segment = jnp.sum(finished.astype(jnp.int32), axis=1)
    offset = jnp.sum(jnp.where(finished, seq_lengths[None, :], 0), axis=1)
    return (segment, indices - offset)


def attend(queries, keypair, query_index, key_index, seq_lengths):
    head_dim = keypair.shape[1] // 2
    row_total = queries.shape[0]
    heads = queries.shape[1] // head_dim
    query_seg = segment_info(query_index, seq_lengths)[0]
    key_seg = segment_info(key_index, seq_lengths)[0]
    allowed = (
        (key_seg[None, :] == query_seg[:, None])
        & (key_index[None, :] <= query_index[:, None])
        & (key_index[None, :] >= 0)
    )
    key_part = keypair[:, :head_dim]
    value_part = keypair[:, head_dim:]

    def one_head(query_rows):
        scores = jnp.dot(query_rows, key_part.T, preferred_element_type=jnp.float32) / math.sqrt(
            head_dim
        )
        masked = jnp.where(allowed, scores, -jnp.inf)
        largest = jnp.max(masked, axis=1, keepdims=True)
        powered = jnp.where(allowed, jnp.exp(masked - largest), 0.0)
        weights = (powered / jnp.sum(powered, axis=1, keepdims=True)).astype(jnp.bfloat16)
        return jnp.dot(weights, value_part, preferred_element_type=jnp.float32).astype(jnp.bfloat16)

    head_major = queries.reshape(row_total, heads, head_dim).transpose(1, 0, 2)
    per_head = lax.map(one_head, head_major)
    return per_head.transpose(1, 0, 2).reshape(row_total, heads * head_dim)


def rotate_queries(query_cols, positions, heads):
    row_total = query_cols.shape[0]
    head_dim = query_cols.shape[1] // heads
    flat = query_cols.astype(jnp.float32).reshape(row_total * heads, head_dim)
    spun = rotated(flat, jnp.repeat(positions, heads))
    return spun.astype(jnp.bfloat16).reshape(row_total, heads * head_dim)


def project_rows(normed, proj):
    return jnp.dot(
        normed,
        lax.all_gather(proj, "fsdp", axis=0, tiled=True).T,
        preferred_element_type=jnp.float32,
    ).astype(jnp.bfloat16)


def per_device(hidden, norm_gain, proj, assign, lengths):
    row_count = hidden.shape[0]
    groups = lax.axis_size("dp")
    per_peer = row_count // groups
    my_group = lax.axis_index("dp")
    column = assign[0]
    group_of = (column // row_count).reshape(groups, row_count)
    slot_of = (column % row_count).reshape(groups, row_count)
    group_ids = jnp.arange(groups, dtype=jnp.int32)
    one_hot = (group_of[:, :, None] == group_ids[None, None, :]).astype(jnp.int32)
    ranking = jnp.sum((jnp.cumsum(one_hot, axis=1) - 1) * one_hot, axis=2)
    buffer_pos = group_of * per_peer + ranking
    own_slots = lax.dynamic_index_in_dim(buffer_pos, my_group, 0, keepdims=False)
    send_index = (
        jnp.zeros((row_count,), jnp.int32).at[own_slots].set(jnp.arange(row_count, dtype=jnp.int32))
    )
    arrival = group_ids[:, None] * per_peer + ranking
    inbound = jnp.where(group_of == my_group, slot_of, row_count)
    place_index = (
        jnp.zeros((row_count,), jnp.int32)
        .at[inbound.reshape(-1)]
        .set(arrival.reshape(-1), mode="drop")
    )
    outbound = jnp.where(group_of == my_group, arrival, row_count)
    return_index = (
        jnp.zeros((row_count,), jnp.int32)
        .at[outbound.reshape(-1)]
        .set(slot_of.reshape(-1), mode="drop")
    )
    outgoing = hidden[send_index].reshape(groups, per_peer, hidden.shape[1])
    arrived = lax.all_to_all(outgoing, "dp", split_axis=0, concat_axis=0, tiled=True)
    working = arrived.reshape(row_count, hidden.shape[1])[place_index]
    projected = project_rows(rms_normed(working, norm_gain), proj)
    head_dim = projected.shape[1] // (QH + 2)
    seq_lengths = lengths[0]
    stream = lax.axis_index("fsdp") * row_count + jnp.arange(row_count, dtype=jnp.int32)
    positions = segment_info(stream, seq_lengths)[1]
    queries = rotate_queries(projected[:, : QH * head_dim], positions, QH)
    keys_rot = rotated(
        projected[:, QH * head_dim : (QH + 1) * head_dim].astype(jnp.float32), positions
    ).astype(jnp.bfloat16)
    keypair = jnp.concatenate([keys_rot, projected[:, (QH + 1) * head_dim :]], axis=1)
    reach_count = lax.axis_size("fsdp") // 2
    levels = reach_count.bit_length()
    window = keypair
    window_index = stream
    for level in range(levels):
        distance = 1 << level
        earlier = from_behind(window, "fsdp", distance)
        window = jnp.concatenate([earlier, window], axis=0)
        window_index = jnp.concatenate([window_index - distance * row_count, window_index], axis=0)
    keep_rows = (reach_count + 1) * row_count
    window = window[window.shape[0] - keep_rows :]
    window_index = window_index[window_index.shape[0] - keep_rows :]
    attended = attend(queries, window, stream, window_index, seq_lengths)
    outgoing_back = attended[return_index].reshape(groups, per_peer, attended.shape[1])
    returned = lax.all_to_all(outgoing_back, "dp", split_axis=0, concat_axis=0, tiled=True)
    return returned.reshape(row_count, attended.shape[1])[own_slots]


def solution(mesh):
    in_specs = (P(("fsdp", "dp"), None), P(), P("fsdp", None), P("fsdp", None), P("dp", None))
    out_specs = P(("fsdp", "dp"), None)
    return jax.shard_map(
        per_device, mesh=mesh, in_specs=in_specs, out_specs=out_specs, check_vma=False
    )
```

profile of v0, /device:TPU:150, one launch (start us, length us, event | category | flops | bytes accessed | tf_op | source)
XLA Modules:
  0.0 778.4 jit_solution(1089616074129539040)
XLA Ops:
  8.1 2.5 select_reduce_fusion
  10.9 1.0 scatter_custom_fusion
  13.4 4.3 scatter_custom_fusion.2
  17.7 3.2 gather_fusion
  20.9 12.3 %all-to-all-start = ((bf16[8,16,8192]{2,1,0:T(8,128)(2,1)}), bf16[8,16,8192]{2,1,0:T(8,128)(2,1)}, u32[]{:S(2)}, u32[]{:S(2)}) async-start(bf16[8,16,8192]{2,1,0:T(8,128)(2,1)} %bitcast.65), calls=%async_computation | async-start | bytes 4194304 | tf_op jit(solution)/shard_map/all_to_all | solution.py:127
  33.5 4.5 scatter_custom_fusion.1
  38.2 70.4 %all-to-all-done = bf16[8,16,8192]{2,1,0:T(8,128)(2,1)} async-done(((bf16[8,16,8192]{2,1,0:T(8,128)(2,1)}), bf16[8,16,8192]{2,1,0:T(8,128)(2,1)}, u32[]{:S(2)}, u32[]{:S(2)}) %all-to-all-start) | async-done | bytes 2097184 | tf_op jit(solution)/shard_map/all_to_all | solution.py:127
  108.7 7.0 gather_fusion.1
  115.6 2.1 fusion.12
  117.7 431.0 %all-gather.2.cloned.1.call-done = bf16[768,8192]{1,0:T(8,128)(2,1)} async-done(((bf16[8,8192]{1,0:T(8,128)(2,1)}), bf16[768,8192]{1,0:T(8,128)(2,1)}) %all-gather.2.cloned.1.call-update) | async-done | bytes 12582928 | tf_op jit(solution)/shard_map/all_gather | solution.py:92
  548.7 8.7 %fusion.19 = bf16[128,768]{0,1:T(8,128)(2,1)S(1)} fusion(bf16[768,8192]{1,0:T(8,128)(2,1)} %all-gather.2.cloned.1.call-done, bf16[128,8192]{1,0:T(8,128)(2,1)} %gather_fusion.1, f32[8192]{0:T(1024)S(1)} %copy-done.8, f32[128]{0:T(128)S(1)} %add_rsqrt_fusion), kind=kOutput, calls=%fused_computation.30 | convolution fusion | flops 1614905344 | bytes 14909952 | tf_op jit(solution)/shard_map/dot_general | solution.py:90
  557.7 4.2 collective-permute-start
  561.8 3.3 collective-permute-done
  565.2 7.7 collective-permute-start.1
  572.9 2.5 collective-permute-done.1
  575.4 11.0 %collective-permute-start.2 = (bf16[512,256]{0,1:T(8,128)(2,1)S(1)}, bf16[512,256]{0,1:T(8,128)(2,1)S(1)}, u32[]{:S(2)}, u32[]{:S(2)}) collective-permute-start(bf16[512,256]{0,1:T(8,128)(2,1)S(1)} %maximum_maximum_fusion.1), channel_id=1, source_target_pairs={{0,32},{8,40},{16,48},{24,56},{32,64},{40,72},{48,80},{56,88},{64,... | collective-permute-start | bytes 786440 | tf_op jit(solution)/shard_map/ppermute | solution.py:18
  586.4 5.7 collective-permute-done.2
  592.1 1.3 collective-permute-start.3
  593.4 15.4 %collective-permute-done.3 = bf16[1024,256]{0,1:T(8,128)(2,1)S(1)} collective-permute-done((bf16[1024,256]{0,1:T(8,128)(2,1)S(1)}, bf16[1024,256]{0,1:T(8,128)(2,1)S(1)}, u32[]{:S(2)}, u32[]{:S(2)}) %collective-permute-start.3) | collective-permute-done | bytes 524320 | tf_op jit(solution)/shard_map/ppermute | solution.py:18
  609.0 1.3 collective-permute-start.4
  610.3 16.8 %collective-permute-done.4 = bf16[2048,256]{0,1:T(8,128)(2,1)S(1)} collective-permute-done((bf16[2048,256]{0,1:T(8,128)(2,1)S(1)}, bf16[2048,256]{0,1:T(8,128)(2,1)S(1)}, u32[]{:S(2)}, u32[]{:S(2)}) %collective-permute-start.4) | collective-permute-done | bytes 1048608 | tf_op jit(solution)/shard_map/ppermute | solution.py:18
  627.2 1.0 copy-done.1
  628.1 1.1 constant_dynamic-update-slice_fusion.10
  632.8 1.5 collective-permute-start.5
  636.5 1.0 reshape.330
  637.5 1.2 fusion.29
  639.0 22.0 %collective-permute-done.5 = bf16[4096,256]{0,1:T(8,128)(2,1)} collective-permute-done((bf16[4096,256]{0,1:T(8,128)(2,1)}, bf16[4096,256]{0,1:T(8,128)(2,1)}, u32[]{:S(2)}, u32[]{:S(2)}) %collective-permute-start.5) | collective-permute-done | bytes 2097184 | tf_op jit(solution)/shard_map/ppermute | solution.py:18
  661.0 1.7 constant_dynamic-update-slice_fusion.17
  663.0 2.0 fusion.55
  664.9 3.7 copy.47
  668.6 3.7 copy.48
  672.3 22.8 %while.11 = (s32[]{:T(128)}, bf16[4,128,128]{2,1,0:T(8,128)(2,1)S(1)}, bf16[4,128,128]{2,1,0:T(8,128)(2,1)S(1)}, bf16[6272,128]{1,0:T(8,128)(2,1)}, bf16[6272,12...) while((s32[]{:T(128)}, ...), condition=%wide.region_12.13_spmd.clone, body=%wide.region_9.12_spmd.clone.sunk | while | flops 428719872 | bytes 19524368 | solution.py:77
  672.3 2.7 fusion.68
  675.1 1.4 fusion.69
  676.5 1.5 fusion.70
  678.0 2.7 fusion.68
  680.8 1.4 fusion.69
  682.2 1.5 fusion.70
  683.7 2.7 fusion.68
  686.5 1.4 fusion.69
  687.9 1.5 fusion.70
  689.4 2.7 fusion.68
  692.2 1.4 fusion.69
  693.6 1.5 fusion.70
  695.2 1.5 gather_fusion.2
  696.7 62.1 %all-to-all-start.1 = ((bf16[8,16,512]{2,1,0:T(8,128)(2,1)}), bf16[8,16,512]{2,1,0:T(8,128)(2,1)S(1)}, u32[]{:S(2)}, u32[]{:S(2)}) async-start(bf16[8,16,512]{2,1,0:T(8,128)(2,1)} %bitcast.17), calls=%async_computation.1 | async-start | bytes 262144 | tf_op jit(solution)/shard_map/all_to_all | solution.py:153
  758.8 11.2 %all-to-all-done.1 = bf16[8,16,512]{2,1,0:T(8,128)(2,1)S(1)} async-done(((bf16[8,16,512]{2,1,0:T(8,128)(2,1)}), bf16[8,16,512]{2,1,0:T(8,128)(2,1)S(1)}, u32[]{:S(2)}, u32[]{:S(2)}) %all-to-all-start.1) | async-done | bytes 131104 | tf_op jit(solution)/shard_map/all_to_all | solution.py:153
  770.0 1.5 gather_fusion.3
  (102 shorter events, 10.6 us)
Async XLA Ops:
  6.5 11.2 %copy-start = (bf16[128,8192]{1,0:T(8,128)(2,1)S(1)}, bf16[128,8192]{1,0:T(8,128)(2,1)}, u32[]{:S(2)}) copy-start(bf16[128,8192]{1,0:T(8,128)(2,1)} %param.7) | copy-start | bytes 6291460
  6.5 542.2 %all-gather.2.cloned.1.call-start = ((), (), s32[]{:S(2)}) async-start(), calls=%async_computation.2 | async-start | bytes 12713984 | tf_op jit(solution)/shard_map/all_gather | solution.py:92
  20.9 12.3 %copy-start.7 = (s32[1,4]{1,0:T(1,128)S(1)}, s32[1,4]{1,0:T(1,128)}, u32[]{:S(2)}) copy-start(s32[1,4]{1,0:T(1,128)} %param.11) | copy-start | bytes 52
  20.9 12.5 %copy-start.6 = (s32[1,1024]{1,0:T(1,128)S(1)}, s32[1,1024]{1,0:T(1,128)}, u32[]{:S(2)}) copy-start(s32[1,1024]{1,0:T(1,128)} %param.10) | copy-start | bytes 12292
  20.9 87.7 %all-to-all-start = ((bf16[8,16,8192]{2,1,0:T(8,128)(2,1)}), bf16[8,16,8192]{2,1,0:T(8,128)(2,1)}, u32[]{:S(2)}, u32[]{:S(2)}) async-start(bf16[8,16,8192]{2,1,0:T(8,128)(2,1)} %bitcast.65), calls=%async_computation | async-start | bytes 4194304 | tf_op jit(solution)/shard_map/all_to_all | solution.py:127
  108.7 440.0 %copy-start.8 = (f32[8192]{0:T(1024)S(1)}, f32[8192]{0:T(1024)}, u32[]{:S(2)}) copy-start(f32[8192]{0:T(1024)} %param.8) | copy-start | bytes 98308
  557.4 71.8 %copy-start.4 = (bf16[128,768]{0,1:T(8,128)(2,1)}, bf16[128,768]{0,1:T(8,128)(2,1)S(1)}, u32[]{:S(2)}) copy-start(bf16[128,768]{0,1:T(8,128)(2,1)S(1)} %fusion.19) | copy-start | bytes 589828
  557.7 7.5 collective-permute-start
  565.2 10.2 %collective-permute-start.1 = (bf16[256,256]{0,1:T(8,128)(2,1)S(1)}, bf16[256,256]{0,1:T(8,128)(2,1)S(1)}, u32[]{:S(2)}, u32[]{:S(2)}) collective-permute-start(bf16[256,256]{0,1:T(8,128)(2,1)S(1)} %maximum_maximum_fusion.2), channel_id=1, source_target_pairs={{0,16},{8,24},{16,32},{24,40},{32,48},{40,56},{48,64},{56,72},{64,... | collective-permute-start | bytes 393224 | tf_op jit(solution)/shard_map/ppermute | solution.py:18
  575.4 16.7 %collective-permute-start.2 = (bf16[512,256]{0,1:T(8,128)(2,1)S(1)}, bf16[512,256]{0,1:T(8,128)(2,1)S(1)}, u32[]{:S(2)}, u32[]{:S(2)}) collective-permute-start(bf16[512,256]{0,1:T(8,128)(2,1)S(1)} %maximum_maximum_fusion.1), channel_id=1, source_target_pairs={{0,32},{8,40},{16,48},{24,56},{32,64},{40,72},{48,80},{56,88},{64,... | collective-permute-start | bytes 786440 | tf_op jit(solution)/shard_map/ppermute | solution.py:18
  592.1 16.7 %collective-permute-start.3 = (bf16[1024,256]{0,1:T(8,128)(2,1)S(1)}, bf16[1024,256]{0,1:T(8,128)(2,1)S(1)}, u32[]{:S(2)}, u32[]{:S(2)}) collective-permute-start(bf16[1024,256]{0,1:T(8,128)(2,1)S(1)} %maximum_maximum_fusion), channel_id=1, source_target_pairs={{0,64},{8,72},{16,80},{24,88},{32,96},{40,104},{48,112},{56,120},{... | collective-permute-start | bytes 1572872 | tf_op jit(solution)/shard_map/ppermute | solution.py:18
  609.0 18.2 %collective-permute-start.4 = (bf16[2048,256]{0,1:T(8,128)(2,1)S(1)}, bf16[2048,256]{0,1:T(8,128)(2,1)S(1)}, u32[]{:S(2)}, u32[]{:S(2)}) collective-permute-start(bf16[2048,256]{0,1:T(8,128)(2,1)S(1)} %constant_dynamic-update-slice_fusion), channel_id=1, source_target_pairs={{0,128},{8,136},{16,144},{24,152},{32,160},{40,168},{48,176},{56,1... | collective-permute-start | bytes 3145736 | tf_op jit(solution)/shard_map/ppermute | solution.py:18
  627.2 1.0 copy-start.1
  632.8 28.2 %collective-permute-start.5 = (bf16[4096,256]{0,1:T(8,128)(2,1)}, bf16[4096,256]{0,1:T(8,128)(2,1)}, u32[]{:S(2)}, u32[]{:S(2)}) collective-permute-start(bf16[4096,256]{0,1:T(8,128)(2,1)} %constant_dynamic-update-slice_fusion.5), channel_id=1, source_target_pairs={{0,256},{8,264},{16,272},{24,280},{32,288},{40,296},{48,304},{56,3... | collective-permute-start | bytes 6291464 | tf_op jit(solution)/shard_map/ppermute | solution.py:18
  637.5 25.2 %copy-start.2 = (bf16[2048,256]{0,1:T(8,128)(2,1)S(1)}, bf16[2048,256]{0,1:T(8,128)(2,1)}, u32[]{:S(2)}) copy-start(bf16[2048,256]{0,1:T(8,128)(2,1)} %copy-done.1) | copy-start | bytes 3145732
  664.9 7.4 copy-start.5
  675.1 1.4 copy-start.3
  680.8 1.4 copy-start.3
  686.5 1.4 copy-start.3
  692.2 1.4 copy-start.3
  696.7 73.4 %all-to-all-start.1 = ((bf16[8,16,512]{2,1,0:T(8,128)(2,1)}), bf16[8,16,512]{2,1,0:T(8,128)(2,1)S(1)}, u32[]{:S(2)}, u32[]{:S(2)}) async-start(bf16[8,16,512]{2,1,0:T(8,128)(2,1)} %bitcast.17), calls=%async_computation.1 | async-start | bytes 262144 | tf_op jit(solution)/shard_map/all_to_all | solution.py:153
Sparse Core Ops, SparseCore 0:
  9.7 538.9 all-gather.1
where the time goes:
time: 780 us; the launch traced here: 778 us
  waiting for transfers between devices  579 us (74%)
  starting transfers between devices  101 us (13%)
  local copies, waits for them, and re-layouts  42.4 us (5%)
  matrix products  25.7 us (3%)
  other arithmetic  15.9 us (2%)
  between operations  13.9 us (2%)
    all_gather x1, waiting for transfers between devices, project_rows(): lax.all_gather(proj, 'fsdp', axis=0, tiled=True)  431 us
    all_to_all x1, waiting for transfers between devices, per_device(): lax.all_to_all(outgoing, 'dp', split_axis=0, concat_axis=0, tiled=True)  70.4 us
    ppermute x6, waiting for transfers between devices, from_behind(): return lax.ppermute(value, axis, pairs)  65.7 us
    all_to_all x1, starting transfers between devices, per_device(): lax.all_to_all(outgoing_back, 'dp', split_axis=0, concat_axis=0, tiled=True)  62.1 us
    ppermute x6, starting transfers between devices, from_behind(): return lax.ppermute(value, axis, pairs)  26.9 us
  transfers between devices with their start and end apart: 9, of which 9 were waited for; matrix products, arithmetic and copies ran while one was open for 4% of the time, Pallas kernels for 0%

commit v1 on v0

--- a/solution.py
+++ b/solution.py
@@ -3,10 +3,12 @@
 import jax
 import jax.numpy as jnp
 from jax import lax
-from jax.sharding import PartitionSpec as P
+from jax.sharding import Mesh, PartitionSpec as P
 
 QH = 4
-
+FSDP = ("zl", "x", "y")
+DP = ("zh", "core")
+SIZES = {"zl": 3, "x": 4, "y": 8, "zh": 4, "core": 2}
 
 THETA = 1000000.0
 EPSILON = 1e-06
@@ -86,19 +88,71 @@
     return spun.astype(jnp.bfloat16).reshape(row_total, heads * head_dim)
 
 
-def project_rows(normed, proj):
-    return jnp.dot(
-        normed,
-        lax.all_gather(proj, "fsdp", axis=0, tiled=True).T,
-        preferred_element_type=jnp.float32,
-    ).astype(jnp.bfloat16)
+def z_shift(value, by):
+    zl_size, zh_size = SIZES["zl"], SIZES["zh"]
+    ring = zl_size * zh_size
+    pairs = []
+    for zl in range(zl_size):
+        for zh in range(zh_size):
+            to = (zh * zl_size + zl + by) % ring
+            pairs.append((zl * zh_size + zh, (to % zl_size) * zh_size + to // zl_size))
+    return lax.ppermute(value, ("zl", "zh"), pairs)
+
+
+def by_class(own, before, after):
+    zl = lax.axis_index("zl")
+    stacked = jnp.stack([own, after, before])
+    return jnp.stack(
+        [
+            lax.dynamic_index_in_dim(stacked, lax.rem(p - zl + 3, 3), 0, keepdims=False)
+            for p in range(3)
+        ]
+    )
+
+
+def spread_x(block):
+    sent = jnp.broadcast_to(block[None], (SIZES["x"],) + block.shape)
+    return lax.all_to_all(sent, "x", 0, 0, tiled=True)
+
+
+def swap_core(value):
+    return lax.ppermute(value, "core", [(0, 1), (1, 0)])
+
+
+def project_home(normed, proj):
+    rows, width = normed.shape
+    core = lax.axis_index("core")
+    half = width // 2
+    mine = lax.dynamic_slice_in_dim(normed, core * half, half, 1)
+    theirs = swap_core(lax.dynamic_slice_in_dim(normed, (1 - core) * half, half, 1))
+    both = jnp.concatenate([mine, theirs], axis=0)
+    shard = lax.dynamic_slice_in_dim(proj, core * half, half, 1)
+    gathered = lax.all_gather(shard, "y", axis=0, tiled=True)
+    cut = (half // 128 * 7 // 16) * 128
+    one = gathered[:, :cut]
+    one = by_class(one, z_shift(one, 1), z_shift(one, -1))
+    one = spread_x(one).transpose(1, 0, 2, 3).reshape(-1, cut)
+    two = spread_x(gathered[:, cut:]).reshape(-1, half - cut)
+    two_before, two_after = z_shift(two, 1), z_shift(two, -1)
+
+    def times(a, w):
+        return lax.dot_general(a, w, (((1,), (1,)), ((), ())), preferred_element_type=jnp.float32)
+
+    sum_one = times(both[:, :cut], one)
+    rest = both[:, cut:]
+    sum_two = by_class(times(rest, two), times(rest, two_before), times(rest, two_after))
+    plane = sum_two.shape[2]
+    total = jnp.concatenate(
+        [sum_two[p] + sum_one[:, p * plane : (p + 1) * plane] for p in range(3)], axis=1
+    )
+    return (total[:rows] + swap_core(total[rows:])).astype(jnp.bfloat16)
 
 
 def per_device(hidden, norm_gain, proj, assign, lengths):
     row_count = hidden.shape[0]
-    groups = lax.axis_size("dp")
+    groups = lax.axis_size(DP)
     per_peer = row_count // groups
-    my_group = lax.axis_index("dp")
+    my_group = lax.axis_index(DP)
     column = assign[0]
     group_of = (column // row_count).reshape(groups, row_count)
     slot_of = (column % row_count).reshape(groups, row_count)
@@ -123,26 +177,26 @@
         .at[outbound.reshape(-1)]
         .set(slot_of.reshape(-1), mode="drop")
     )
-    outgoing = hidden[send_index].reshape(groups, per_peer, hidden.shape[1])
-    arrived = lax.all_to_all(outgoing, "dp", split_axis=0, concat_axis=0, tiled=True)
-    working = arrived.reshape(row_count, hidden.shape[1])[place_index]
-    projected = project_rows(rms_normed(working, norm_gain), proj)
+    home = project_home(rms_normed(hidden, norm_gain), proj)
+    outgoing = home[send_index].reshape(groups, per_peer, home.shape[1])
+    arrived = lax.all_to_all(outgoing, DP, split_axis=0, concat_axis=0, tiled=True)
+    projected = arrived.reshape(row_count, home.shape[1])[place_index]
     head_dim = projected.shape[1] // (QH + 2)
     seq_lengths = lengths[0]
-    stream = lax.axis_index("fsdp") * row_count + jnp.arange(row_count, dtype=jnp.int32)
+    stream = lax.axis_index(FSDP) * row_count + jnp.arange(row_count, dtype=jnp.int32)
     positions = segment_info(stream, seq_lengths)[1]
     queries = rotate_queries(projected[:, : QH * head_dim], positions, QH)
     keys_rot = rotated(
         projected[:, QH * head_dim : (QH + 1) * head_dim].astype(jnp.float32), positions
     ).astype(jnp.bfloat16)
     keypair = jnp.concatenate([keys_rot, projected[:, (QH + 1) * head_dim :]], axis=1)
-    reach_count = lax.axis_size("fsdp") // 2
+    reach_count = lax.axis_size(FSDP) // 2
     levels = reach_count.bit_length()
     window = keypair
     window_index = stream
     for level in range(levels):
         distance = 1 << level
-        earlier = from_behind(window, "fsdp", distance)
+        earlier = from_behind(window, FSDP, distance)
         window = jnp.concatenate([earlier, window], axis=0)
         window_index = jnp.concatenate([window_index - distance * row_count, window_index], axis=0)
     keep_rows = (reach_count + 1) * row_count
@@ -150,13 +204,14 @@
     window_index = window_index[window_index.shape[0] - keep_rows :]
     attended = attend(queries, window, stream, window_index, seq_lengths)
     outgoing_back = attended[return_index].reshape(groups, per_peer, attended.shape[1])
-    returned = lax.all_to_all(outgoing_back, "dp", split_axis=0, concat_axis=0, tiled=True)
+    returned = lax.all_to_all(outgoing_back, DP, split_axis=0, concat_axis=0, tiled=True)
     return returned.reshape(row_count, attended.shape[1])[own_slots]
 
 
 def solution(mesh):
-    in_specs = (P(("fsdp", "dp"), None), P(), P("fsdp", None), P("fsdp", None), P("dp", None))
-    out_specs = P(("fsdp", "dp"), None)
+    shape = [SIZES[name] for name in FSDP + DP]
+    fine = Mesh(mesh.devices.reshape(shape), FSDP + DP)
+    in_specs = (P(FSDP + DP, None), P(), P(FSDP, None), P(FSDP, None), P(DP, None))
     return jax.shard_map(
-        per_device, mesh=mesh, in_specs=in_specs, out_specs=out_specs, check_vma=False
-    )
+        per_device, mesh=fine, in_specs=in_specs, out_specs=P(FSDP + DP, None), check_vma=False
+    )

time: 780 us -> 330 us (0.42)
  the two profiles are of different devices: /device:TPU:150 before, /device:TPU:64 now
where the time goes in v1:
time: 330 us; the launch traced here: 329 us
  waiting for transfers between devices  162 us (49%)
  starting transfers between devices  65.7 us (20%)
  local copies, waits for them, and re-layouts  33.7 us (10%)
  blocking collectives  26.9 us (8%)
  matrix products  22.1 us (7%)
  other arithmetic  17.2 us (5%)
    ppermute x6, waiting for transfers between devices, from_behind(): return lax.ppermute(value, axis, pairs)  102 us
    all_gather x1, blocking collectives, project_home(): gathered = lax.all_gather(shard, 'y', axis=0, tiled=True)  26.9 us
    ppermute x4, waiting for transfers between devices, z_shift(): return lax.ppermute(value, ('zl', 'zh'), pairs)  20.9 us
    ppermute x4, starting transfers between devices, z_shift(): return lax.ppermute(value, ('zl', 'zh'), pairs)  20.6 us
    ppermute x6, starting transfers between devices, from_behind(): return lax.ppermute(value, axis, pairs)  15.6 us
    all_to_all x1, waiting for transfers between devices, per_device(): lax.all_to_all(outgoing, DP, split_axis=0, concat_axis=0, tiled=True)  13.4 us
    all_to_all x2, waiting for transfers between devices, spread_x(): return lax.all_to_all(sent, 'x', 0, 0, tiled=True)  12.4 us
    all_to_all x1, waiting for transfers between devices, per_device(): lax.all_to_all(outgoing_back, DP, split_axis=0, concat_axis=0, tiled=True)  12 us
  transfers between devices with their start and end apart: 16, of which 12 were waited for; matrix products, arithmetic and copies ran while one was open for 11% of the time, Pallas kernels for 0%

profile of v1, /device:TPU:64, one launch (start us, length us, event | category | flops | bytes accessed | tf_op | source)
XLA Modules:
  0.0 328.9 jit_solution(17801555081456977862)
XLA Ops:
  0.9 26.9 %all_gather.3 = bf16[64,4096]{1,0:T(8,128)(2,1)S(1)} all-gather(bf16[8,4096]{1,0:T(8,128)(2,1)S(1)} %constant_dynamic-slice_fusion.6), channel_id=1, replica_groups=mesh['zl'=3,'x'=4,'y'=8,'zh'=4,'core'=2] {'y'}, dimensions={0}, use_global_device_ids=true | all-gather | bytes 589824 | tf_op jit(solution)/shard_map/all_gather | solution.py:130
  27.9 9.0 %collective-permute-start.3 = (bf16[64,1792]{1,0:T(8,128)(2,1)S(1)}, bf16[64,1792]{1,0:T(8,128)(2,1)S(1)}, u32[]{:S(2)}, u32[]{:S(2)}) collective-permute-start(bf16[64,1792]{1,0:T(8,128)(2,1)S(1)} %get-tuple-element.155), channel_id=1, source_target_pairs={{0,518},{2,512},{4,514},{6,516},{256,0},{258,2},{260,4},{262,6},{5... | collective-permute-start | bytes 688136 | tf_op jit(solution)/shard_map/ppermute | solution.py:99
  36.9 1.9 collective-permute-start.4
  38.9 2.1 fusion.12
  43.1 2.0 collective-permute-start
  46.3 3.5 %all-to-all-start = ((bf16[4,64,2304]{2,1,0:T(8,128)(2,1)}), bf16[4,64,2304]{2,1,0:T(8,128)(2,1)S(1)}, u32[]{:S(2)}, u32[]{:S(2)}) async-start(bf16[4,64,2304]{2,1,0:T(8,128)(2,1)} %broadcast_in_dim.41), calls=%async_computation | async-start | bytes 2359296 | tf_op jit(solution)/shard_map/all_to_all | solution.py:115
  50.1 2.5 select_reduce_fusion
  54.9 12.4 %all-to-all-done = bf16[4,64,2304]{2,1,0:T(8,128)(2,1)S(1)} async-done(((bf16[4,64,2304]{2,1,0:T(8,128)(2,1)}), bf16[4,64,2304]{2,1,0:T(8,128)(2,1)S(1)}, u32[]{:S(2)}, u32[]{:S(2)}) %all-to-all-start) | async-done | bytes 1179680 | tf_op jit(solution)/shard_map/all_to_all | solution.py:115
  67.3 1.9 broadcast_in_dim.42
  69.2 3.8 %all-to-all-start.1 = ((bf16[4,3,64,1792]{3,2,1,0:T(8,128)(2,1)}), bf16[4,3,64,1792]{3,2,1,0:T(8,128)(2,1)S(1)}, u32[]{:S(2)}, u32[]{:S(2)}) async-start(bf16[4,3,64,1792]{3,2,1,0:T(8,128)(2,1)} %broadcast_in_dim.42), calls=%async_computation.1 | async-start | bytes 5505024 | tf_op jit(solution)/shard_map/all_to_all | solution.py:115
  73.0 1.9 collective-permute-start.2
  76.1 4.3 %scatter_custom_fusion.1 = s32[128]{0:T(128)S(1)} fusion(s32[1024]{0:T(1024)S(1)} %bitcast.99, s32[1024]{0:T(1024)S(1)} %fusion.64, s32[]{:T(128)} %copy.98), kind=kCustom, calls=%fused_computation.173 | custom fusion | bytes 516 | tf_op jit(solution)/shard_map/scatter | solution.py:172
  80.5 7.7 %collective-permute-start.1 = (bf16[256,2304]{1,0:T(8,128)(2,1)}, bf16[256,2304]{1,0:T(8,128)(2,1)S(1)}, u32[]{:S(2)}, u32[]{:S(2)}) collective-permute-start(bf16[256,2304]{1,0:T(8,128)(2,1)} %bitcast.91), channel_id=1, source_target_pairs={{0,518},{2,512},{4,514},{6,516},{256,0},{258,2},{260,4},{262,6},{5... | collective-permute-start | bytes 3538952 | tf_op jit(solution)/shard_map/ppermute | solution.py:99
  88.3 2.1 convolution_bitcast_fusion.2
  90.5 16.0 %collective-permute-done.2 = bf16[256,2304]{1,0:T(8,128)(2,1)} collective-permute-done((bf16[256,2304]{1,0:T(8,128)(2,1)}, bf16[256,2304]{1,0:T(8,128)(2,1)}, u32[]{:S(2)}, u32[]{:S(2)}) %collective-permute-start.2) | collective-permute-done | bytes 1179680 | tf_op jit(solution)/shard_map/ppermute | solution.py:99
  106.5 2.0 convolution_bitcast_fusion
  108.4 4.9 %collective-permute-done.1 = bf16[256,2304]{1,0:T(8,128)(2,1)S(1)} collective-permute-done((bf16[256,2304]{1,0:T(8,128)(2,1)}, bf16[256,2304]{1,0:T(8,128)(2,1)S(1)}, u32[]{:S(2)}, u32[]{:S(2)}) %collective-permute-start.1) | collective-permute-done | bytes 1179680 | tf_op jit(solution)/shard_map/ppermute | solution.py:99
  113.3 1.6 convolution_bitcast_fusion.1
  117.1 1.8 copy.47
  120.1 2.0 fusion.16
  122.3 1.9 collective-permute-start.5
  124.3 1.6 collective-permute-done.5
  126.0 1.6 gather_fusion
  127.5 8.1 %all-to-all-start.2 = ((bf16[8,16,768]{2,1,0:T(8,128)(2,1)}), bf16[8,16,768]{2,1,0:T(8,128)(2,1)S(1)}, u32[]{:S(2)}, u32[]{:S(2)}) async-start(bf16[8,16,768]{2,1,0:T(8,128)(2,1)} %bitcast.14), calls=%async_computation.2 | async-start | bytes 393216 | tf_op jit(solution)/shard_map/all_to_all | solution.py:182
  136.2 13.4 %all-to-all-done.2 = bf16[8,16,768]{2,1,0:T(8,128)(2,1)S(1)} async-done(((bf16[8,16,768]{2,1,0:T(8,128)(2,1)}), bf16[8,16,768]{2,1,0:T(8,128)(2,1)S(1)}, u32[]{:S(2)}, u32[]{:S(2)}) %all-to-all-start.2) | async-done | bytes 196640 | tf_op jit(solution)/shard_map/all_to_all | solution.py:182
  151.2 2.7 collective-permute-start.6
  153.9 7.6 %collective-permute-done.6 = bf16[128,256]{1,0:T(8,128)(2,1)S(1)} collective-permute-done((bf16[128,256]{1,0:T(8,128)(2,1)S(1)}, bf16[128,256]{1,0:T(8,128)(2,1)S(1)}, u32[]{:S(2)}, u32[]{:S(2)}) %collective-permute-start.6) | collective-permute-done | bytes 65568 | tf_op jit(solution)/shard_map/ppermute | solution.py:20
  161.7 1.9 collective-permute-start.7
  163.6 10.1 %collective-permute-done.7 = bf16[256,256]{1,0:T(8,128)(2,1)S(1)} collective-permute-done((bf16[256,256]{1,0:T(8,128)(2,1)S(1)}, bf16[256,256]{1,0:T(8,128)(2,1)S(1)}, u32[]{:S(2)}, u32[]{:S(2)}) %collective-permute-start.7) | collective-permute-done | bytes 131104 | tf_op jit(solution)/shard_map/ppermute | solution.py:20
  173.7 1.9 collective-permute-start.8
  175.7 15.3 %collective-permute-done.8 = bf16[512,256]{1,0:T(8,128)(2,1)S(1)} collective-permute-done((bf16[512,256]{1,0:T(8,128)(2,1)S(1)}, bf16[512,256]{1,0:T(8,128)(2,1)S(1)}, u32[]{:S(2)}, u32[]{:S(2)}) %collective-permute-start.8) | collective-permute-done | bytes 262176 | tf_op jit(solution)/shard_map/ppermute | solution.py:20
  191.1 1.9 collective-permute-start.9
  193.0 12.1 %collective-permute-done.9 = bf16[1024,256]{1,0:T(8,128)(2,1)S(1)} collective-permute-done((bf16[1024,256]{1,0:T(8,128)(2,1)S(1)}, bf16[1024,256]{1,0:T(8,128)(2,1)S(1)}, u32[]{:S(2)}, u32[]{:S(2)}) %collective-permute-start.9) | collective-permute-done | bytes 524320 | tf_op jit(solution)/shard_map/ppermute | solution.py:20
  205.3 2.7 collective-permute-start.10
  208.1 21.7 %collective-permute-done.10 = bf16[2048,256]{1,0:T(8,128)(2,1)S(1)} collective-permute-done((bf16[2048,256]{1,0:T(8,128)(2,1)S(1)}, bf16[2048,256]{1,0:T(8,128)(2,1)S(1)}, u32[]{:S(2)}, u32[]{:S(2)}) %collective-permute-start.10) | collective-permute-done | bytes 1048608 | tf_op jit(solution)/shard_map/ppermute | solution.py:20
  234.5 4.4 %collective-permute-start.11 = (bf16[4096,256]{1,0:T(8,128)(2,1)}, bf16[4096,256]{1,0:T(8,128)(2,1)}, u32[]{:S(2)}, u32[]{:S(2)}) collective-permute-start(bf16[4096,256]{1,0:T(8,128)(2,1)} %constant_dynamic-update-slice_fusion.5), channel_id=1, source_target_pairs={{0,256},{8,264},{16,272},{24,280},{32,288},{40,296},{48,304},{56,3... | collective-permute-start | bytes 6291464 | tf_op jit(solution)/shard_map/ppermute | solution.py:20
  239.2 4.4 %scatter_custom_fusion.2 = s32[128]{0:T(128)S(1)} fusion(s32[1024]{0:T(1024)} %bitcast.100, s32[1024]{0:T(1024)S(1)} %add_select_fusion.1, s32[]{:T(128)} %copy.98), kind=kCustom, calls=%fused_computation.171 | custom fusion | bytes 1024 | tf_op jit(solution)/shard_map/scatter | solution.py:178
  246.0 35.1 %collective-permute-done.11 = bf16[4096,256]{1,0:T(8,128)(2,1)} collective-permute-done((bf16[4096,256]{1,0:T(8,128)(2,1)}, bf16[4096,256]{1,0:T(8,128)(2,1)}, u32[]{:S(2)}, u32[]{:S(2)}) %collective-permute-start.11) | collective-permute-done | bytes 2097184 | tf_op jit(solution)/shard_map/ppermute | solution.py:20
  281.1 1.7 constant_dynamic-update-slice_fusion.17
  283.7 20.0 %while.11 = (s32[]{:T(128)}, bf16[4,128,128]{2,1,0:T(8,128)(2,1)S(1)}, bf16[4,128,128]{2,1,0:T(8,128)(2,1)}, bf16[6272,128]{1,0:T(8,128)(2,1)S(1)}, bf16[6272,12...) while((s32[]{:T(128)}, ...), condition=%wide.region_12.13_spmd.clone, body=%wide.region_9.12_spmd.clone.sunk | while | flops 428719872 | bytes 13094257 | solution.py:79
  283.7 2.0 fusion.73
  287.1 1.6 fusion.75
  288.7 2.1 fusion.73
  292.1 1.6 fusion.75
  293.7 2.1 fusion.73
  298.7 2.1 fusion.73
  305.2 10.1 %all-to-all-start.3 = ((bf16[8,16,512]{2,1,0:T(8,128)(2,1)}), bf16[8,16,512]{2,1,0:T(8,128)(2,1)S(1)}, u32[]{:S(2)}, u32[]{:S(2)}) async-start(bf16[8,16,512]{2,1,0:T(8,128)(2,1)} %bitcast.29), calls=%async_computation.3 | async-start | bytes 262144 | tf_op jit(solution)/shard_map/all_to_all | solution.py:207
  315.4 12.0 %all-to-all-done.3 = bf16[8,16,512]{2,1,0:T(8,128)(2,1)S(1)} async-done(((bf16[8,16,512]{2,1,0:T(8,128)(2,1)}), bf16[8,16,512]{2,1,0:T(8,128)(2,1)S(1)}, u32[]{:S(2)}, u32[]{:S(2)}) %all-to-all-start.3) | async-done | bytes 131104 | tf_op jit(solution)/shard_map/all_to_all | solution.py:207
  (149 shorter events, 33.7 us)
Async XLA Ops:
  0.0 0.9 copy-start
  0.0 40.9 %copy-start.1 = (bf16[128,8192]{1,0:T(8,128)(2,1)S(1)}, bf16[128,8192]{1,0:T(8,128)(2,1)}, u32[]{:S(2)}) copy-start(bf16[128,8192]{1,0:T(8,128)(2,1)} %param.7) | copy-start | bytes 6291460
  0.0 41.0 %copy-start.7 = (f32[8192]{0:T(1024)S(1)}, f32[8192]{0:T(1024)}, u32[]{:S(2)}) copy-start(f32[8192]{0:T(1024)} %param.8) | copy-start | bytes 98308
  27.9 25.8 %collective-permute-start.3 = (bf16[64,1792]{1,0:T(8,128)(2,1)S(1)}, bf16[64,1792]{1,0:T(8,128)(2,1)S(1)}, u32[]{:S(2)}, u32[]{:S(2)}) collective-permute-start(bf16[64,1792]{1,0:T(8,128)(2,1)S(1)} %get-tuple-element.155), channel_id=1, source_target_pairs={{0,518},{2,512},{4,514},{6,516},{256,0},{258,2},{260,4},{262,6},{5... | collective-permute-start | bytes 688136 | tf_op jit(solution)/shard_map/ppermute | solution.py:99
  36.9 16.8 %collective-permute-start.4 = (bf16[64,1792]{1,0:T(8,128)(2,1)S(1)}, bf16[64,1792]{1,0:T(8,128)(2,1)}, u32[]{:S(2)}, u32[]{:S(2)}) collective-permute-start(bf16[64,1792]{1,0:T(8,128)(2,1)S(1)} %get-tuple-element.155), channel_id=1, source_target_pairs={{0,256},{2,258},{4,260},{6,262},{256,512},{258,514},{260,516},{262... | collective-permute-start | bytes 688136 | tf_op jit(solution)/shard_map/ppermute | solution.py:99
  43.1 6.8 %copy-start.6 = (s32[1,1024]{1,0:T(1,128)S(1)}, s32[1,1024]{1,0:T(1,128)}, u32[]{:S(2)}) copy-start(s32[1,1024]{1,0:T(1,128)} %param.10) | copy-start | bytes 12292
  43.1 45.2 %collective-permute-start = (bf16[128,4096]{1,0:T(8,128)(2,1)}, bf16[128,4096]{1,0:T(8,128)(2,1)}, u32[]{:S(2)}, u32[]{:S(2)}) collective-permute-start(bf16[128,4096]{1,0:T(8,128)(2,1)} %get-tuple-element.144), channel_id=1, source_target_pairs={{0,1},{1,0},{2,3},{3,2},{4,5},{5,4},{6,7},{7,6},{8,9},{9,8},{10,11... | collective-permute-start | bytes 3145736 | tf_op jit(solution)/shard_map/ppermute | solution.py:119
  46.3 20.9 %all-to-all-start = ((bf16[4,64,2304]{2,1,0:T(8,128)(2,1)}), bf16[4,64,2304]{2,1,0:T(8,128)(2,1)S(1)}, u32[]{:S(2)}, u32[]{:S(2)}) async-start(bf16[4,64,2304]{2,1,0:T(8,128)(2,1)} %broadcast_in_dim.41), calls=%async_computation | async-start | bytes 2359296 | tf_op jit(solution)/shard_map/all_to_all | solution.py:115
  67.3 1.9 copy-start.4
  69.2 5.8 %copy-start.13 = (s32[1,4]{1,0:T(1,128)S(1)}, s32[1,4]{1,0:T(1,128)}, u32[]{:S(2)}) copy-start(s32[1,4]{1,0:T(1,128)} %param.11) | copy-start | bytes 52
  69.2 49.7 %all-to-all-start.1 = ((bf16[4,3,64,1792]{3,2,1,0:T(8,128)(2,1)}), bf16[4,3,64,1792]{3,2,1,0:T(8,128)(2,1)S(1)}, u32[]{:S(2)}, u32[]{:S(2)}) async-start(bf16[4,3,64,1792]{3,2,1,0:T(8,128)(2,1)} %broadcast_in_dim.42), calls=%async_computation.1 | async-start | bytes 5505024 | tf_op jit(solution)/shard_map/all_to_all | solution.py:115
  73.0 17.5 %copy-start.14 = (s32[128]{0:T(128)}, s32[128]{0:T(128)S(1)}, u32[]{:S(2)}) copy-start(s32[128]{0:T(128)S(1)} %fusion.44) | copy-start | bytes 1540
  73.0 33.5 %collective-permute-start.2 = (bf16[256,2304]{1,0:T(8,128)(2,1)}, bf16[256,2304]{1,0:T(8,128)(2,1)}, u32[]{:S(2)}, u32[]{:S(2)}) collective-permute-start(bf16[256,2304]{1,0:T(8,128)(2,1)} %bitcast.90), channel_id=1, source_target_pairs={{0,256},{2,258},{4,260},{6,262},{256,512},{258,514},{260,516},{262... | collective-permute-start | bytes 3538952 | tf_op jit(solution)/shard_map/ppermute | solution.py:99
  75.1 60.5 %copy-start.11 = (s32[4,1]{0,1:T(1,128)}, s32[4,1]{0,1:T(1,128)S(1)}, u32[]{:S(2)}) copy-start(s32[4,1]{0,1:T(1,128)S(1)} %reduce-window.8) | copy-start | bytes 52
  80.4 26.0 %copy-start.2 = (bf16[128,4096]{1,0:T(8,128)(2,1)S(1)}, bf16[128,4096]{1,0:T(8,128)(2,1)}, u32[]{:S(2)}) copy-start(bf16[128,4096]{1,0:T(8,128)(2,1)} %get-tuple-element.143) | copy-start | bytes 3145732
  80.5 32.8 %collective-permute-start.1 = (bf16[256,2304]{1,0:T(8,128)(2,1)}, bf16[256,2304]{1,0:T(8,128)(2,1)S(1)}, u32[]{:S(2)}, u32[]{:S(2)}) collective-permute-start(bf16[256,2304]{1,0:T(8,128)(2,1)} %bitcast.91), channel_id=1, source_target_pairs={{0,518},{2,512},{4,514},{6,516},{256,0},{258,2},{260,4},{262,6},{5... | collective-permute-start | bytes 3538952 | tf_op jit(solution)/shard_map/ppermute | solution.py:99
  88.2 119.8 %copy-start.8 = (s32[512]{0:T(512)}, s32[512]{0:T(512)S(1)}, u32[]{:S(2)}) copy-start(s32[512]{0:T(512)S(1)} %add_add_fusion.1) | copy-start | bytes 6148
  118.9 1.2 copy-start.3
  120.1 2.0 copy-start.5
  122.3 3.6 %collective-permute-start.5 = (f32[128,768]{1,0:T(8,128)S(1)}, f32[128,768]{1,0:T(8,128)S(1)}, u32[]{:S(2)}, u32[]{:S(2)}) collective-permute-start(f32[128,768]{1,0:T(8,128)S(1)} %slice.95), channel_id=1, source_target_pairs={{0,1},{1,0},{2,3},{3,2},{4,5},{5,4},{6,7},{7,6},{8,9},{9,8},{10,11... | collective-permute-start | bytes 1179656 | tf_op jit(solution)/shard_map/ppermute | solution.py:119
  127.5 22.1 %all-to-all-start.2 = ((bf16[8,16,768]{2,1,0:T(8,128)(2,1)}), bf16[8,16,768]{2,1,0:T(8,128)(2,1)S(1)}, u32[]{:S(2)}, u32[]{:S(2)}) async-start(bf16[8,16,768]{2,1,0:T(8,128)(2,1)} %bitcast.14), calls=%async_computation.2 | async-start | bytes 393216 | tf_op jit(solution)/shard_map/all_to_all | solution.py:182
  151.2 10.4 %collective-permute-start.6 = (bf16[128,256]{1,0:T(8,128)(2,1)S(1)}, bf16[128,256]{1,0:T(8,128)(2,1)S(1)}, u32[]{:S(2)}, u32[]{:S(2)}) collective-permute-start(bf16[128,256]{1,0:T(8,128)(2,1)S(1)} %pad_maximum_fusion.6), channel_id=1, source_target_pairs={{0,8},{8,16},{16,24},{24,32},{32,40},{40,48},{48,56},{56,64},{64,7... | collective-permute-start | bytes 196616 | tf_op jit(solution)/shard_map/ppermute | solution.py:20
  161.7 12.0 %collective-permute-start.7 = (bf16[256,256]{1,0:T(8,128)(2,1)S(1)}, bf16[256,256]{1,0:T(8,128)(2,1)S(1)}, u32[]{:S(2)}, u32[]{:S(2)}) collective-permute-start(bf16[256,256]{1,0:T(8,128)(2,1)S(1)} %maximum_maximum_fusion.2), channel_id=1, source_target_pairs={{0,16},{8,24},{16,32},{24,40},{32,48},{40,56},{48,64},{56,72},{64,... | collective-permute-start | bytes 393224 | tf_op jit(solution)/shard_map/ppermute | solution.py:20
  173.7 17.3 %collective-permute-start.8 = (bf16[512,256]{1,0:T(8,128)(2,1)S(1)}, bf16[512,256]{1,0:T(8,128)(2,1)S(1)}, u32[]{:S(2)}, u32[]{:S(2)}) collective-permute-start(bf16[512,256]{1,0:T(8,128)(2,1)S(1)} %maximum_maximum_fusion.1), channel_id=1, source_target_pairs={{0,32},{8,40},{16,48},{24,56},{32,64},{40,72},{48,80},{56,88},{64,... | collective-permute-start | bytes 786440 | tf_op jit(solution)/shard_map/ppermute | solution.py:20
  191.1 14.0 %collective-permute-start.9 = (bf16[1024,256]{1,0:T(8,128)(2,1)S(1)}, bf16[1024,256]{1,0:T(8,128)(2,1)S(1)}, u32[]{:S(2)}, u32[]{:S(2)}) collective-permute-start(bf16[1024,256]{1,0:T(8,128)(2,1)S(1)} %maximum_maximum_fusion), channel_id=1, source_target_pairs={{0,64},{8,72},{16,80},{24,88},{32,96},{40,104},{48,112},{56,120},{... | collective-permute-start | bytes 1572872 | tf_op jit(solution)/shard_map/ppermute | solution.py:20
  205.2 38.5 %copy-start.12 = (s32[4,1]{0,1:T(1,128)S(1)}, s32[4,1]{0,1:T(1,128)}, u32[]{:S(2)}) copy-start(s32[4,1]{0,1:T(1,128)} %copy-done.11) | copy-start | bytes 52
  205.3 24.6 %collective-permute-start.10 = (bf16[2048,256]{1,0:T(8,128)(2,1)S(1)}, bf16[2048,256]{1,0:T(8,128)(2,1)S(1)}, u32[]{:S(2)}, u32[]{:S(2)}) collective-permute-start(bf16[2048,256]{1,0:T(8,128)(2,1)S(1)} %constant_dynamic-update-slice_fusion), channel_id=1, source_target_pairs={{0,128},{8,136},{16,144},{24,152},{32,160},{40,168},{48,176},{56,1... | collective-permute-start | bytes 3145736 | tf_op jit(solution)/shard_map/ppermute | solution.py:20
  208.1 31.0 %copy-start.9 = (s32[512]{0:T(512)S(1)}, s32[512]{0:T(512)}, u32[]{:S(2)}) copy-start(s32[512]{0:T(512)} %copy-done.8) | copy-start | bytes 6148
  234.5 46.6 %collective-permute-start.11 = (bf16[4096,256]{1,0:T(8,128)(2,1)}, bf16[4096,256]{1,0:T(8,128)(2,1)}, u32[]{:S(2)}, u32[]{:S(2)}) collective-permute-start(bf16[4096,256]{1,0:T(8,128)(2,1)} %constant_dynamic-update-slice_fusion.5), channel_id=1, source_target_pairs={{0,256},{8,264},{16,272},{24,280},{32,288},{40,296},{48,304},{56,3... | collective-permute-start | bytes 6291464 | tf_op jit(solution)/shard_map/ppermute | solution.py:20
  283.1 0.6 copy-start.10
  283.7 31.7 %copy-start.15 = (s32[128]{0:T(128)S(1)}, s32[128]{0:T(128)}, u32[]{:S(2)}) copy-start(s32[128]{0:T(128)} %copy-done.14) | copy-start | bytes 1540
  305.2 22.1 %all-to-all-start.3 = ((bf16[8,16,512]{2,1,0:T(8,128)(2,1)}), bf16[8,16,512]{2,1,0:T(8,128)(2,1)S(1)}, u32[]{:S(2)}, u32[]{:S(2)}) async-start(bf16[8,16,512]{2,1,0:T(8,128)(2,1)} %bitcast.29), calls=%async_computation.3 | async-start | bytes 262144 | tf_op jit(solution)/shard_map/all_to_all | solution.py:207

commit v2 on v1

v2 whole, which is shorter than its diff:
```python
import functools
import math

import jax
import jax.numpy as jnp
from jax import lax
from jax.experimental import pallas as pl
from jax.experimental.pallas import tpu as pltpu
from jax.sharding import Mesh, PartitionSpec as P

QH = 4
FSDP = ("zl", "x", "y")
DP = ("zh", "core")
SIZES = {"zl": 3, "x": 4, "y": 8, "zh": 4, "core": 2}

THETA = 1000000.0
EPSILON = 1e-06


def rms_normed(block_rows, norm_gain):
    widened = block_rows.astype(jnp.float32)
    inverse = lax.rsqrt(jnp.mean(widened * widened, axis=1, keepdims=True) + EPSILON)
    return (widened * inverse * norm_gain).astype(jnp.bfloat16)


def rope_tables(positions, width):
    half_width = width // 2
    inverse_freq = THETA ** (-(jnp.arange(half_width, dtype=jnp.float32) * 2.0) / width)
    angles = positions.astype(jnp.float32)[:, None] * inverse_freq[None, :]
    cosine, sine = jnp.cos(angles), jnp.sin(angles)
    return jnp.concatenate([cosine, cosine], axis=1), jnp.concatenate([-sine, sine], axis=1)


def segment_info(indices, seq_lengths):
    ends_at = jnp.cumsum(seq_lengths)
    finished = ends_at[None, :] <= indices[:, None]
    segment = jnp.sum(finished.astype(jnp.int32), axis=1)
    offset = jnp.sum(jnp.where(finished, seq_lengths[None, :], 0), axis=1)
    return (segment, indices - offset, offset)


def z_shift(value, by):
    zl_size, zh_size = SIZES["zl"], SIZES["zh"]
    ring = zl_size * zh_size
    pairs = []
    for zl in range(zl_size):
        for zh in range(zh_size):
            to = (zh * zl_size + zl + by) % ring
            pairs.append((zl * zh_size + zh, (to % zl_size) * zh_size + to // zl_size))
    return lax.ppermute(value, ("zl", "zh"), pairs)


def spread(block, axis):
    sent = jnp.broadcast_to(block[None], (SIZES[axis],) + block.shape)
    return lax.all_to_all(sent, axis, 0, 0, tiled=True)


def swap_core(value):
    return lax.ppermute(value, "core", [(0, 1), (1, 0)])


def kernel_call(body, outs, scalars, flops, operands):
    spaces = [pltpu.SMEM] * scalars + [pltpu.VMEM] * (len(operands) - scalars)
    moved = sum(a.size * a.dtype.itemsize for a in list(operands) + list(outs))
    return pl.pallas_call(
        body,
        out_shape=outs,
        in_specs=[pl.BlockSpec(memory_space=space) for space in spaces],
        out_specs=[pl.BlockSpec(memory_space=pltpu.VMEM)] * len(outs),
        compiler_params=pltpu.CompilerParams(vmem_limit_bytes=40 * 1024 * 1024),
        cost_estimate=pl.CostEstimate(flops=flops, bytes_accessed=moved, transcendentals=0),
    )(*operands)


def dot(a, b):
    return jnp.dot(a, b, preferred_element_type=jnp.float32)


def dot_t(a, b):
    return lax.dot_general(a, b, (((1,), (1,)), ((), ())), preferred_element_type=jnp.float32)


def pack_body(zl_ref, mine_ref, other_ref, order_ref, out_ref):
    third = out_ref.shape[1] // 3
    zl = zl_ref[0]
    for p in range(3):
        k = lax.rem(p - zl + 3, 3)
        cols = pl.ds(pl.multiple_of(k * third, third), third)
        rounded = (mine_ref[:, cols] + other_ref[:, cols]).astype(jnp.bfloat16)
        out_ref[:, p * third : (p + 1) * third] = dot(order_ref[...], rounded).astype(jnp.bfloat16)


def unpack_body(arrived_ref, place_ref, cos_ref, sin_ref, q_ref, kv_ref):
    rows = arrived_ref.shape[0]
    hd = cos_ref.shape[1]
    placed = dot(place_ref[...], arrived_ref[...])
    cosine, sine = cos_ref[...], sin_ref[...]

    def rope(h):
        x = placed[:, h * hd : (h + 1) * hd]
        return (x * cosine + pltpu.roll(x, hd // 2, 1) * sine).astype(jnp.bfloat16)

    for h in range(QH):
        q_ref[h * rows : (h + 1) * rows, :] = rope(h)
    kv_ref[:, :hd] = rope(QH)
    kv_ref[:, hd:] = placed[:, (QH + 1) * hd :].astype(jnp.bfloat16)


def attend_body(parts, first, last, stride, *refs):
    base_ref, start_ref, q_ref = refs[:3]
    kv_refs = refs[3 : 3 + parts]
    at = 3 + parts
    if not first:
        m_in, l_in, acc_in = refs[at : at + 3]
        at += 3
    if last:
        back_ref, out_ref = refs[at : at + 2]
    else:
        m_out, l_out, acc_out = refs[at : at + 3]
    rows = start_ref.shape[0]
    hd = q_ref.shape[1]
    scale = math.log2(math.e) / math.sqrt(hd)
    start = start_ref[...]
    query = base_ref[parts] * rows + lax.broadcasted_iota(jnp.int32, (rows, 1), 0)
    allowed = []
    for i, kv_ref in enumerate(kv_refs):
        n = kv_ref.shape[0]
        col = lax.broadcasted_iota(jnp.int32, (1, n), 1)
        key = base_ref[i] * rows + (col % rows) - (col // rows) * (stride * rows)
        allowed.append((key >= start) & (key <= query))
    done = []
    for h in range(QH):
        at_rows = slice(h * rows, (h + 1) * rows)
        q = q_ref[at_rows, :]
        scores = [
            jnp.where(ok, dot_t(q, kv_ref[:, :hd]), -jnp.inf) for ok, kv_ref in zip(allowed, kv_refs)
        ]
        largest = functools.reduce(
            jnp.maximum, [jnp.max(s, axis=1, keepdims=True) for s in scores]
        )
        if not first:
            m_old = m_in[at_rows, :][:, :1]
            largest = jnp.maximum(largest, m_old)
        total, acc = 0.0, 0.0
        for s, kv_ref in zip(scores, kv_refs):
            p = jnp.exp2((s - largest) * scale)
            total = total + jnp.sum(p, axis=1, keepdims=True)
            acc = acc + dot(p.astype(jnp.bfloat16), kv_ref[:, hd:])
        if not first:
            shrink = jnp.exp2((m_old - largest) * scale)
            total = total + l_in[at_rows, :][:, :1] * shrink
            acc = acc + acc_in[at_rows, :] * shrink
        if last:
            done.append((acc / total).astype(jnp.bfloat16))
        else:
            m_out[at_rows, :] = jnp.broadcast_to(largest, (rows, hd))
            l_out[at_rows, :] = jnp.broadcast_to(total, (rows, hd))
            acc_out[at_rows, :] = acc
    if last:
        for h in range(QH):
            out_ref[:, h * hd : (h + 1) * hd] = dot(back_ref[...], done[h]).astype(jnp.bfloat16)


def attend(queries, start, kv_parts, bases, own, stride, state=None, back=None):
    total, hd = queries.shape
    rows = total // QH
    scalars = jnp.stack([*bases, own]).astype(jnp.int32)
    operands = [scalars, start, queries, *kv_parts]
    if state is not None:
        operands += list(state)
    if back is not None:
        operands.append(back)
        outs = [jax.ShapeDtypeStruct((rows, total // rows * hd), jnp.bfloat16)]
    else:
        outs = [jax.ShapeDtypeStruct((total, hd), jnp.float32)] * 3
    keys = sum(part.shape[0] for part in kv_parts)
    body = functools.partial(
        attend_body, len(kv_parts), state is None, back is not None, stride
    )
    return kernel_call(body, outs, 1, 16 * total * keys * hd, operands)


def project_halves(normed, proj):
    rows, width = normed.shape
    core = lax.axis_index("core")
    half = width // 2
    shard = lax.dynamic_slice_in_dim(proj, core * half, half, 1)
    gathered = spread(shard, "y").reshape(-1, half)
    mine = lax.dynamic_slice_in_dim(normed, core * half, half, 1)
    theirs = swap_core(lax.dynamic_slice_in_dim(normed, (1 - core) * half, half, 1))
    gathered, mine, theirs = lax.optimization_barrier((gathered, mine, theirs))
    both = jnp.concatenate([mine, theirs], axis=0)
    cut = (half // 128 * 7 // 16) * 128
    two = spread(gathered[:, cut:], "x").reshape(-1, half - cut)
    one = gathered[:, :cut]
    one = jnp.stack([one, z_shift(one, -1), z_shift(one, 1)])
    two_before, two_after = z_shift(two, 1), z_shift(two, -1)
    one = spread(one, "x").transpose(1, 0, 2, 3).reshape(-1, cut)
    sum_one = dot_t(both[:, :cut], one)
    rest = both[:, cut:]
    sum_two = jnp.concatenate(
        [dot_t(rest, two), dot_t(rest, two_after), dot_t(rest, two_before)], axis=1
    )
    total = sum_one + sum_two
    return total[:rows], swap_core(total[rows:])


def one_hot_rows(target, count):
    return (target[None, :] == jnp.arange(count, dtype=jnp.int32)[:, None]).astype(jnp.bfloat16)


def per_device(hidden, norm_gain, proj, assign, lengths):
    row_count = hidden.shape[0]
    groups = lax.axis_size(DP)
    per_peer = row_count // groups
    my_group = lax.axis_index(DP)
    mine, other = project_halves(rms_normed(hidden, norm_gain), proj)
    column = assign[0]
    group_of = (column // row_count).reshape(groups, row_count)
    slot_of = (column % row_count).reshape(groups, row_count)
    row_ids = jnp.arange(row_count, dtype=jnp.int32)
    own_group = lax.dynamic_index_in_dim(group_of, my_group, 0, keepdims=False)
    same = (own_group[:, None] == own_group[None, :]) & (row_ids[None, :] < row_ids[:, None])
    own_slots = own_group * per_peer + jnp.sum(same.astype(jnp.int32), axis=1)
    to_me = group_of == my_group
    earlier = to_me[:, None, :] & (row_ids[None, None, :] < row_ids[None, :, None])
    rank = jnp.sum(earlier.astype(jnp.int32), axis=2)
    ranks = jnp.arange(per_peer, dtype=jnp.int32)
    hit = to_me[:, None, :] & (rank[:, None, :] == ranks[None, :, None])
    slot_at = jnp.sum(jnp.where(hit, slot_of[:, None, :], 0), axis=2).reshape(row_count)
    send_order = one_hot_rows(own_slots, row_count)
    place_order = one_hot_rows(slot_at, row_count)

    stream_id = lax.axis_index(FSDP)
    stream = stream_id * row_count + row_ids
    _, positions, starts = segment_info(stream, lengths[0])
    width = mine.shape[1]
    head_dim = width // (QH + 2)
    cosine, sine = rope_tables(positions, head_dim)

    zl = lax.axis_index("zl")
    bf16 = jnp.bfloat16
    outgoing = kernel_call(
        pack_body,
        [jax.ShapeDtypeStruct((row_count, width), bf16)],
        1,
        2 * row_count * row_count * width,
        [zl[None].astype(jnp.int32), mine, other, send_order],
    )[0]
    arrived = lax.all_to_all(
        outgoing.reshape(groups, per_peer, width), DP, split_axis=0, concat_axis=0, tiled=True
    ).reshape(row_count, width)
    queries, keypair = kernel_call(
        unpack_body,
        [
            jax.ShapeDtypeStruct((QH * row_count, head_dim), bf16),
            jax.ShapeDtypeStruct((row_count, 2 * head_dim), bf16),
        ],
        0,
        2 * row_count * row_count * width,
        [arrived, place_order, cosine, sine],
    )

    ring = SIZES["y"]
    peers = lax.axis_size(FSDP)
    depth = peers // 2 // ring
    blocks = [keypair]
    for j in range(1, depth + 1):
        pairs = [(i, i + j * ring) for i in range(peers - j * ring)]
        blocks.append(lax.ppermute(keypair, FSDP, pairs))
    column_blocks = jnp.concatenate(blocks, axis=0)
    start = starts[:, None]
    state = attend(queries, start, [column_blocks], [stream_id], stream_id, ring)
    y = lax.axis_index("y")
    forward, backward = column_blocks[: depth * row_count], column_blocks
    step_up = [(i, i + 1) for i in range(peers - 1)]
    step_down = [(i, (i - 1) % ring) for i in range(ring)]
    for step in range(1, ring // 2 + 1):
        forward = lax.ppermute(forward, FSDP, step_up)
        parts, bases = [forward], [stream_id - step]
        if step < ring // 2:
            backward = lax.ppermute(backward, "y", step_down)
            parts.append(backward)
            bases.append(stream_id - y + lax.rem(y + step, ring))
            state = attend(queries, start, parts, bases, stream_id, ring, state)
        else:
            outgoing_back = attend(
                queries, start, parts, bases, stream_id, ring, state, place_order.T
            )[0]
    returned = lax.all_to_all(
        outgoing_back.reshape(groups, per_peer, -1), DP, split_axis=0, concat_axis=0, tiled=True
    ).reshape(row_count, -1)
    return lax.dot_general(
        send_order, returned, (((0,), (0,)), ((), ())), preferred_element_type=jnp.float32
    ).astype(bf16)


def solution(mesh):
    shape = [SIZES[name] for name in FSDP + DP]
    fine = Mesh(mesh.devices.reshape(shape), FSDP + DP)
    in_specs = (P(FSDP + DP, None), P(), P(FSDP, None), P(FSDP, None), P(DP, None))
    return jax.shard_map(
        per_device, mesh=fine, in_specs=in_specs, out_specs=P(FSDP + DP, None), check_vma=False
    )
```

time: 330 us -> 232 us (0.70)
  the two profiles are of different devices: /device:TPU:64 before, /device:TPU:128 now
where the time goes in v2:
time: 232 us; the launch traced here: 231 us
  waiting for transfers between devices  104 us (45%)
  starting transfers between devices  73.2 us (32%)
  blocking collectives  19.5 us (8%)
  Pallas kernels  14.6 us (6%)
  local copies, waits for them, and re-layouts  8.9 us (4%)
  other arithmetic  5.52 us (2%)
  matrix products  5.21 us (2%)
    ppermute x4, waiting for transfers between devices, z_shift(): return lax.ppermute(value, ('zl', 'zh'), pairs)  31.6 us
    ppermute x4, waiting for transfers between devices, per_device(): forward = lax.ppermute(forward, FSDP, step_up)  29.2 us
    all_to_all x3, waiting for transfers between devices, spread(): return lax.all_to_all(sent, axis, 0, 0, tiled=True)  20.6 us
    all_to_all x1, blocking collectives, per_device(): lax.all_to_all(outgoing_back.reshape(groups, per_peer, -1), DP, split_axi...  19.5 us
    ppermute x4, starting transfers between devices, z_shift(): return lax.ppermute(value, ('zl', 'zh'), pairs)  15.5 us
    all_to_all x3, starting transfers between devices, spread(): return lax.all_to_all(sent, axis, 0, 0, tiled=True)  15.1 us
    pallas_call x7, Pallas kernels, kernel_call(): pl.pallas_call(body, out_shape=outs, in_specs=[pl.BlockSpec(memory_space=...  14.6 us
    all_to_all x1, waiting for transfers between devices, per_device(): lax.all_to_all(outgoing.reshape(groups, per_peer, width), DP, split_axis=...  14 us
  transfers between devices with their start and end apart: 23, of which 15 were waited for; matrix products, arithmetic and copies ran while one was open for 3% of the time, Pallas kernels for 5%

profile of v2, /device:TPU:128, one launch (start us, length us, event | category | flops | bytes accessed | tf_op | source)
XLA Modules:
  0.0 231.3 jit_solution(3626847509264823877)
XLA Ops:
  0.0 2.2 fusion
  2.3 1.4 fusion.2
  4.9 1.9 collective-permute-start
  7.7 7.1 %all-to-all-start = ((bf16[8,8,4096]{2,1,0:T(8,128)(2,1)}), bf16[8,8,4096]{2,1,0:T(8,128)(2,1)S(1)}, u32[]{:S(2)}, u32[]{:S(2)}) async-start(bf16[8,8,4096]{2,1,0:T(8,128)(2,1)} %broadcast_in_dim.37), calls=%async_computation | async-start | bytes 1048576 | tf_op jit(solution)/shard_map/all_to_all | solution.py:55
  15.5 17.5 %all-to-all-done = bf16[8,8,4096]{2,1,0:T(8,128)(2,1)S(1)} async-done(((bf16[8,8,4096]{2,1,0:T(8,128)(2,1)}), bf16[8,8,4096]{2,1,0:T(8,128)(2,1)S(1)}, u32[]{:S(2)}, u32[]{:S(2)}) %all-to-all-start) | async-done | bytes 524320 | tf_op jit(solution)/shard_map/all_to_all | solution.py:55
  34.3 4.3 %all-to-all-start.2 = ((bf16[4,64,2304]{2,1,0:T(8,128)(2,1)}), bf16[4,64,2304]{2,1,0:T(8,128)(2,1)S(1)}, u32[]{:S(2)}, u32[]{:S(2)}) async-start(bf16[4,64,2304]{2,1,0:T(8,128)(2,1)} %broadcast_in_dim.39), calls=%async_computation.2 | async-start | bytes 2359296 | tf_op jit(solution)/shard_map/all_to_all | solution.py:55
  38.6 1.9 collective-permute-start.1
  40.6 4.3 %collective-permute-start.2 = (bf16[64,1792]{1,0:T(8,128)(2,1)S(1)}, bf16[64,1792]{1,0:T(8,128)(2,1)S(1)}, u32[]{:S(2)}, u32[]{:S(2)}) collective-permute-start(bf16[64,1792]{1,0:T(8,128)(2,1)S(1)} %get-tuple-element.46), channel_id=1, source_target_pairs={{0,256},{2,258},{4,260},{6,262},{256,512},{258,514},{260,516},{262... | collective-permute-start | bytes 688136 | tf_op jit(solution)/shard_map/ppermute | solution.py:50
  45.1 3.3 %collective-permute-done.1 = bf16[64,1792]{1,0:T(8,128)(2,1)S(1)} collective-permute-done((bf16[64,1792]{1,0:T(8,128)(2,1)S(1)}, bf16[64,1792]{1,0:T(8,128)(2,1)S(1)}, u32[]{:S(2)}, u32[]{:S(2)}) %collective-permute-start.1) | collective-permute-done | bytes 229408 | tf_op jit(solution)/shard_map/ppermute | solution.py:50
  48.5 3.7 %collective-permute-done.2 = bf16[64,1792]{1,0:T(8,128)(2,1)S(1)} collective-permute-done((bf16[64,1792]{1,0:T(8,128)(2,1)S(1)}, bf16[64,1792]{1,0:T(8,128)(2,1)S(1)}, u32[]{:S(2)}, u32[]{:S(2)}) %collective-permute-start.2) | collective-permute-done | bytes 229408 | tf_op jit(solution)/shard_map/ppermute | solution.py:50
  52.3 3.1 %all-to-all-done.2 = bf16[4,64,2304]{2,1,0:T(8,128)(2,1)S(1)} async-done(((bf16[4,64,2304]{2,1,0:T(8,128)(2,1)}), bf16[4,64,2304]{2,1,0:T(8,128)(2,1)S(1)}, u32[]{:S(2)}, u32[]{:S(2)}) %all-to-all-start.2) | async-done | bytes 1179680 | tf_op jit(solution)/shard_map/all_to_all | solution.py:55
  55.3 1.9 broadcast_in_dim.38
  57.2 3.7 %all-to-all-start.1 = ((bf16[4,3,64,1792]{3,2,1,0:T(8,128)(2,1)}), bf16[4,3,64,1792]{3,2,1,0:T(8,128)(2,1)S(1)}, u32[]{:S(2)}, u32[]{:S(2)}) async-start(bf16[4,3,64,1792]{3,2,1,0:T(8,128)(2,1)} %broadcast_in_dim.38), calls=%async_computation.1 | async-start | bytes 5505024 | tf_op jit(solution)/shard_map/all_to_all | solution.py:55
  61.0 7.4 %collective-permute-start.3 = (bf16[256,2304]{1,0:T(8,128)(2,1)}, bf16[256,2304]{1,0:T(8,128)(2,1)S(1)}, u32[]{:S(2)}, u32[]{:S(2)}) collective-permute-start(bf16[256,2304]{1,0:T(8,128)(2,1)} %bitcast.45), channel_id=1, source_target_pairs={{0,518},{2,512},{4,514},{6,516},{256,0},{258,2},{260,4},{262,6},{5... | collective-permute-start | bytes 3538952 | tf_op jit(solution)/shard_map/ppermute | solution.py:50
  68.4 1.9 collective-permute-start.4
  70.3 1.3 constant_dynamic-update-slice_fusion.1
  72.2 20.1 %collective-permute-done.3 = bf16[256,2304]{1,0:T(8,128)(2,1)S(1)} collective-permute-done((bf16[256,2304]{1,0:T(8,128)(2,1)}, bf16[256,2304]{1,0:T(8,128)(2,1)S(1)}, u32[]{:S(2)}, u32[]{:S(2)}) %collective-permute-start.3) | collective-permute-done | bytes 1179680 | tf_op jit(solution)/shard_map/ppermute | solution.py:50
  92.8 4.4 %collective-permute-done.4 = bf16[256,2304]{1,0:T(8,128)(2,1)S(1)} collective-permute-done((bf16[256,2304]{1,0:T(8,128)(2,1)}, bf16[256,2304]{1,0:T(8,128)(2,1)S(1)}, u32[]{:S(2)}, u32[]{:S(2)}) %collective-permute-start.4) | collective-permute-done | bytes 1179680 | tf_op jit(solution)/shard_map/ppermute | solution.py:50
  99.5 2.1 fusion.5
  101.6 1.9 collective-permute-start.5
  103.6 1.7 collective-permute-done.5.other_ref
  106.1 9.4 %all-to-all-start.3 = ((bf16[8,16,768]{2,1,0:T(8,128)(2,1)}), bf16[8,16,768]{2,1,0:T(8,128)(2,1)S(1)}, u32[]{:S(2)}, u32[]{:S(2)}) async-start(bf16[8,16,768]{2,1,0:T(8,128)(2,1)} %bitcast.18), calls=%async_computation.3 | async-start | bytes 393216 | tf_op jit(solution)/shard_map/all_to_all | solution.py:250
  116.1 14.0 %all-to-all-done.3 = bf16[8,16,768]{2,1,0:T(8,128)(2,1)S(1)} async-done(((bf16[8,16,768]{2,1,0:T(8,128)(2,1)}), bf16[8,16,768]{2,1,0:T(8,128)(2,1)S(1)}, u32[]{:S(2)}, u32[]{:S(2)}) %all-to-all-start.3) | async-done | bytes 196640 | tf_op jit(solution)/shard_map/all_to_all | solution.py:250
  130.4 3.6 %collective-permute-start.6 = (bf16[128,256]{1,0:T(8,128)(2,1)S(1)}, bf16[128,256]{1,0:T(8,128)(2,1)S(1)}, u32[]{:S(2)}, u32[]{:S(2)}) collective-permute-start(bf16[128,256]{1,0:T(8,128)(2,1)S(1)} %get-tuple-element.26), channel_id=1, source_target_pairs={{0,64},{8,72},{16,80},{24,88},{32,96},{40,104},{48,112},{56,120},{... | collective-permute-start | bytes 196616 | tf_op jit(solution)/shard_map/ppermute | solution.py:270
  134.0 4.6 %collective-permute-start.7 = (bf16[128,256]{1,0:T(8,128)(2,1)S(1)}, bf16[128,256]{1,0:T(8,128)(2,1)S(1)}, u32[]{:S(2)}, u32[]{:S(2)}) collective-permute-start(bf16[128,256]{1,0:T(8,128)(2,1)S(1)} %get-tuple-element.26), channel_id=1, source_target_pairs={{0,128},{8,136},{16,144},{24,152},{32,160},{40,168},{48,176},{56,1... | collective-permute-start | bytes 196616 | tf_op jit(solution)/shard_map/ppermute | solution.py:270
  138.6 1.9 collective-permute-start.8
  140.5 1.3 collective-permute-start.9
  141.8 1.3 collective-permute-start.10
  144.5 1.8 collective-permute-done.8
  146.3 1.4 collective-permute-done.9
  147.7 3.6 %collective-permute-done.10 = bf16[128,256]{1,0:T(8,128)(2,1)S(1)} collective-permute-done((bf16[128,256]{1,0:T(8,128)(2,1)S(1)}, bf16[128,256]{1,0:T(8,128)(2,1)S(1)}, u32[]{:S(2)}, u32[]{:S(2)}) %collective-permute-start.10) | collective-permute-done | bytes 65568 | tf_op jit(solution)/shard_map/ppermute | solution.py:270
  151.4 1.9 collective-permute-start.11
  153.3 3.7 %collective-permute-start.16 = (bf16[896,256]{1,0:T(8,128)(2,1)S(1)}, bf16[896,256]{1,0:T(8,128)(2,1)S(1)}, u32[]{:S(2)}, u32[]{:S(2)}) collective-permute-start(bf16[896,256]{1,0:T(8,128)(2,1)S(1)} %constant_dynamic-update-slice_fusion.8.refs_3_), channel_id=1, source_target_pairs={{0,56},{8,0},{16,8},{24,16},{32,24},{40,32},{48,40},{56,48},{1,57}... | collective-permute-start | bytes 1376264 | tf_op jit(solution)/shard_map/ppermute | solution.py:282
  157.0 9.1 %collective-permute-done.11.refs_3_ = bf16[768,256]{1,0:T(8,128)(2,1)S(1)} collective-permute-done((bf16[768,256]{1,0:T(8,128)(2,1)S(1)}, bf16[768,256]{1,0:T(8,128)(2,1)S(1)}, u32[]{:S(2)}, u32[]{:S(2)}) %collective-permute-start.11) | collective-permute-done | bytes 393248 | tf_op jit(solution)/shard_map/ppermute | solution.py:279
  166.2 1.9 collective-permute-start.12
  168.1 1.9 collective-permute-start.17
  170.2 9.8 %collective-permute-done.12.refs_3_ = bf16[768,256]{1,0:T(8,128)(2,1)S(1)} collective-permute-done((bf16[768,256]{1,0:T(8,128)(2,1)S(1)}, bf16[768,256]{1,0:T(8,128)(2,1)S(1)}, u32[]{:S(2)}, u32[]{:S(2)}) %collective-permute-start.12) | collective-permute-done | bytes 393248 | tf_op jit(solution)/shard_map/ppermute | solution.py:279
  180.0 1.9 collective-permute-start.13
  182.1 1.9 collective-permute-start.18
  185.1 2.1 shard_map.57
  187.3 6.7 %collective-permute-done.13.refs_3_ = bf16[768,256]{1,0:T(8,128)(2,1)S(1)} collective-permute-done((bf16[768,256]{1,0:T(8,128)(2,1)S(1)}, bf16[768,256]{1,0:T(8,128)(2,1)S(1)}, u32[]{:S(2)}, u32[]{:S(2)}) %collective-permute-start.13) | collective-permute-done | bytes 393248 | tf_op jit(solution)/shard_map/ppermute | solution.py:279
  193.9 2.1 collective-permute-start.14
  196.0 3.0 %shard_map.58 = (f32[512,128]{1,0:T(8,128)S(1)}, f32[512,128]{1,0:T(8,128)S(1)}, f32[512,128]{1,0:T(8,128)S(1)}) custom-call(s32[3]{0:T(128)S(1)} %add_add_fusion.2.refs_0_, s32[128,1]{1,0:T(8,128)S(1)} %copy.39.refs_1_, bf16[512,128]{1,0:T(8,128)(2,1)S(1)} %copy-done.2, bf16[768,256]{1,0:T(8,128)(2,1)S(1)} %collective-permute-done.11.refs_3_, ...), custom_call_target="tpu_custom_call" | custom-call | flops 1744830464 | bytes 2556428 | tf_op jit(solution)/shard_map/pallas_call | solution.py:65
  199.0 3.0 %shard_map.59 = (f32[512,128]{1,0:T(8,128)S(1)}, f32[512,128]{1,0:T(8,128)S(1)}, f32[512,128]{1,0:T(8,128)S(1)}) custom-call(s32[3]{0:T(128)S(1)} %add_add_fusion.1.refs_0_, s32[128,1]{1,0:T(8,128)S(1)} %copy.39.refs_1_, bf16[512,128]{1,0:T(8,128)(2,1)S(1)} %copy-done.2, bf16[768,256]{1,0:T(8,128)(2,1)S(1)} %collective-permute-done.12.refs_3_, ...), custom_call_target="tpu_custom_call" | custom-call | flops 1744830464 | bytes 2556428 | tf_op jit(solution)/shard_map/pallas_call | solution.py:65
  201.9 3.0 %shard_map.60 = (f32[512,128]{1,0:T(8,128)S(1)}, f32[512,128]{1,0:T(8,128)S(1)}, f32[512,128]{1,0:T(8,128)S(1)}) custom-call(s32[3]{0:T(128)S(1)} %add_add_fusion.refs_0_, s32[128,1]{1,0:T(8,128)S(1)} %copy.39.refs_1_, bf16[512,128]{1,0:T(8,128)(2,1)S(1)} %copy-done.2, bf16[768,256]{1,0:T(8,128)(2,1)S(1)} %collective-permute-done.13.refs_3_, ...), custom_call_target="tpu_custom_call" | custom-call | flops 1744830464 | bytes 2556428 | tf_op jit(solution)/shard_map/pallas_call | solution.py:65
  205.0 3.5 %collective-permute-done.14.refs_3_ = bf16[768,256]{1,0:T(8,128)(2,1)S(1)} collective-permute-done((bf16[768,256]{1,0:T(8,128)(2,1)S(1)}, bf16[768,256]{1,0:T(8,128)(2,1)S(1)}, u32[]{:S(2)}, u32[]{:S(2)}) %collective-permute-start.14) | collective-permute-done | bytes 393248 | tf_op jit(solution)/shard_map/ppermute | solution.py:279
  208.5 2.4 %shard_map.61 = bf16[128,512]{1,0:T(8,128)(2,1)S(1)} custom-call(s32[2]{0:T(128)S(1)} %pad_add_fusion.refs_0_, s32[128,1]{1,0:T(8,128)S(1)} %copy.39.refs_1_, bf16[512,128]{1,0:T(8,128)(2,1)S(1)} %copy-done.2, bf16[768,256]{1,0:T(8,128)(2,1)S(1)} %collective-permute-done.14.refs_3_, f32[512,128]{1,0:T(8,128)S(1)} %get-tuple-element.36.refs_4_, ...), custom_call_target="tpu_custom_call" | custom-call | flops 805306368 | bytes 1475080 | tf_op jit(solution)/shard_map/pallas_call | solution.py:65
  210.9 19.5 %all_to_all.25 = bf16[8,16,512]{2,1,0:T(8,128)(2,1)S(1)} all-to-all(bf16[8,16,512]{2,1,0:T(8,128)(2,1)S(1)} %bitcast.41), channel_id=1, replica_groups=mesh['zl'=3,'x'=4,'y'=8,'zh'=4,'core'=2] {'zh','core'}, dimensions={0} | all-to-all | bytes 262144 | tf_op jit(solution)/shard_map/all_to_all | solution.py:290
  (81 shorter events, 13.2 us)
Async XLA Ops:
  0.0 6.8 %copy-start = (bf16[8,8192]{1,0:T(8,128)(2,1)S(1)}, bf16[8,8192]{1,0:T(8,128)(2,1)}, u32[]{:S(2)}) copy-start(bf16[8,8192]{1,0:T(8,128)(2,1)} %param.7) | copy-start | bytes 393220
  0.0 2.3 copy-start.3
  3.7 11.1 %copy-start.10 = (s32[1,4]{1,0:T(1,128)S(1)}, s32[1,4]{1,0:T(1,128)}, u32[]{:S(2)}) copy-start(s32[1,4]{1,0:T(1,128)} %param.9) | copy-start | bytes 52
  3.7 11.3 %copy-start.9 = (s32[1,1024]{1,0:T(1,128)S(1)}, s32[1,1024]{1,0:T(1,128)}, u32[]{:S(2)}) copy-start(s32[1,1024]{1,0:T(1,128)} %param.8) | copy-start | bytes 12292
  4.9 28.1 %collective-permute-start = (bf16[128,4096]{1,0:T(8,128)(2,1)S(1)}, bf16[128,4096]{1,0:T(8,128)(2,1)S(1)}, u32[]{:S(2)}, u32[]{:S(2)}) collective-permute-start(bf16[128,4096]{1,0:T(8,128)(2,1)S(1)} %get-tuple-element.41), channel_id=1, source_target_pairs={{0,1},{1,0},{2,3},{3,2},{4,5},{5,4},{6,7},{7,6},{8,9},{9,8},{10,11... | collective-permute-start | bytes 3145736 | tf_op jit(solution)/shard_map/ppermute | solution.py:59
  7.7 25.3 %all-to-all-start = ((bf16[8,8,4096]{2,1,0:T(8,128)(2,1)}), bf16[8,8,4096]{2,1,0:T(8,128)(2,1)S(1)}, u32[]{:S(2)}, u32[]{:S(2)}) async-start(bf16[8,8,4096]{2,1,0:T(8,128)(2,1)} %broadcast_in_dim.37), calls=%async_computation | async-start | bytes 1048576 | tf_op jit(solution)/shard_map/all_to_all | solution.py:55
  33.0 1.4 copy-start.6
  34.3 21.0 %all-to-all-start.2 = ((bf16[4,64,2304]{2,1,0:T(8,128)(2,1)}), bf16[4,64,2304]{2,1,0:T(8,128)(2,1)S(1)}, u32[]{:S(2)}, u32[]{:S(2)}) async-start(bf16[4,64,2304]{2,1,0:T(8,128)(2,1)} %broadcast_in_dim.39), calls=%async_computation.2 | async-start | bytes 2359296 | tf_op jit(solution)/shard_map/all_to_all | solution.py:55
  38.6 9.8 %collective-permute-start.1 = (bf16[64,1792]{1,0:T(8,128)(2,1)S(1)}, bf16[64,1792]{1,0:T(8,128)(2,1)S(1)}, u32[]{:S(2)}, u32[]{:S(2)}) collective-permute-start(bf16[64,1792]{1,0:T(8,128)(2,1)S(1)} %get-tuple-element.46), channel_id=1, source_target_pairs={{0,518},{2,512},{4,514},{6,516},{256,0},{258,2},{260,4},{262,6},{5... | collective-permute-start | bytes 688136 | tf_op jit(solution)/shard_map/ppermute | solution.py:50
  40.6 11.6 %collective-permute-start.2 = (bf16[64,1792]{1,0:T(8,128)(2,1)S(1)}, bf16[64,1792]{1,0:T(8,128)(2,1)S(1)}, u32[]{:S(2)}, u32[]{:S(2)}) collective-permute-start(bf16[64,1792]{1,0:T(8,128)(2,1)S(1)} %get-tuple-element.46), channel_id=1, source_target_pairs={{0,256},{2,258},{4,260},{6,262},{256,512},{258,514},{260,516},{262... | collective-permute-start | bytes 688136 | tf_op jit(solution)/shard_map/ppermute | solution.py:50
  55.3 1.9 copy-start.4
  57.2 41.3 %all-to-all-start.1 = ((bf16[4,3,64,1792]{3,2,1,0:T(8,128)(2,1)}), bf16[4,3,64,1792]{3,2,1,0:T(8,128)(2,1)S(1)}, u32[]{:S(2)}, u32[]{:S(2)}) async-start(bf16[4,3,64,1792]{3,2,1,0:T(8,128)(2,1)} %broadcast_in_dim.38), calls=%async_computation.1 | async-start | bytes 5505024 | tf_op jit(solution)/shard_map/all_to_all | solution.py:55
  61.0 10.6 %copy-start.7 = (bf16[128,4096]{1,0:T(8,128)(2,1)S(1)}, bf16[128,4096]{1,0:T(8,128)(2,1)}, u32[]{:S(2)}) copy-start(bf16[128,4096]{1,0:T(8,128)(2,1)} %copy-done.6) | copy-start | bytes 3145732
  61.0 10.7 %copy-start.5 = (bf16[4,64,2304]{2,1,0:T(8,128)(2,1)S(1)}, bf16[4,64,2304]{2,1,0:T(8,128)(2,1)}, u32[]{:S(2)}) copy-start(bf16[4,64,2304]{2,1,0:T(8,128)(2,1)} %copy-done.4) | copy-start | bytes 3538948
  61.0 31.3 %collective-permute-start.3 = (bf16[256,2304]{1,0:T(8,128)(2,1)}, bf16[256,2304]{1,0:T(8,128)(2,1)S(1)}, u32[]{:S(2)}, u32[]{:S(2)}) collective-permute-start(bf16[256,2304]{1,0:T(8,128)(2,1)} %bitcast.45), channel_id=1, source_target_pairs={{0,518},{2,512},{4,514},{6,516},{256,0},{258,2},{260,4},{262,6},{5... | collective-permute-start | bytes 3538952 | tf_op jit(solution)/shard_map/ppermute | solution.py:50
  68.4 28.9 %collective-permute-start.4 = (bf16[256,2304]{1,0:T(8,128)(2,1)}, bf16[256,2304]{1,0:T(8,128)(2,1)S(1)}, u32[]{:S(2)}, u32[]{:S(2)}) collective-permute-start(bf16[256,2304]{1,0:T(8,128)(2,1)} %bitcast.46), channel_id=1, source_target_pairs={{0,256},{2,258},{4,260},{6,262},{256,512},{258,514},{260,516},{262... | collective-permute-start | bytes 3538952 | tf_op jit(solution)/shard_map/ppermute | solution.py:50
  71.7 25.6 %copy-start.8 = (bf16[256,4096]{1,0:T(8,128)(2,1)}, bf16[256,4096]{1,0:T(8,128)(2,1)S(1)}, u32[]{:S(2)}) copy-start(bf16[256,4096]{1,0:T(8,128)(2,1)S(1)} %constant_dynamic-update-slice_fusion) | copy-start | bytes 6291460
  98.5 1.0 copy-start.11
  101.6 3.6 %collective-permute-start.5 = (f32[128,768]{1,0:T(8,128)S(1)}, f32[128,768]{1,0:T(8,128)S(1)}, u32[]{:S(2)}, u32[]{:S(2)}) collective-permute-start(f32[128,768]{1,0:T(8,128)S(1)} %get-tuple-element.43), channel_id=1, source_target_pairs={{0,1},{1,0},{2,3},{3,2},{4,5},{5,4},{6,7},{7,6},{8,9},{9,8},{10,11... | collective-permute-start | bytes 1179656 | tf_op jit(solution)/shard_map/ppermute | solution.py:59
  106.1 24.0 %all-to-all-start.3 = ((bf16[8,16,768]{2,1,0:T(8,128)(2,1)}), bf16[8,16,768]{2,1,0:T(8,128)(2,1)S(1)}, u32[]{:S(2)}, u32[]{:S(2)}) async-start(bf16[8,16,768]{2,1,0:T(8,128)(2,1)} %bitcast.18), calls=%async_computation.3 | async-start | bytes 393216 | tf_op jit(solution)/shard_map/all_to_all | solution.py:250
  130.4 37.7 %copy-start.1 = (bf16[512,128]{1,0:T(8,128)(2,1)}, bf16[512,128]{1,0:T(8,128)(2,1)S(1)}, u32[]{:S(2)}) copy-start(bf16[512,128]{1,0:T(8,128)(2,1)S(1)} %get-tuple-element.25.refs_2_) | copy-start | bytes 393220
  130.4 12.8 %collective-permute-start.6 = (bf16[128,256]{1,0:T(8,128)(2,1)S(1)}, bf16[128,256]{1,0:T(8,128)(2,1)S(1)}, u32[]{:S(2)}, u32[]{:S(2)}) collective-permute-start(bf16[128,256]{1,0:T(8,128)(2,1)S(1)} %get-tuple-element.26), channel_id=1, source_target_pairs={{0,64},{8,72},{16,80},{24,88},{32,96},{40,104},{48,112},{56,120},{... | collective-permute-start | bytes 196616 | tf_op jit(solution)/shard_map/ppermute | solution.py:270
  134.0 10.5 %collective-permute-start.7 = (bf16[128,256]{1,0:T(8,128)(2,1)S(1)}, bf16[128,256]{1,0:T(8,128)(2,1)S(1)}, u32[]{:S(2)}, u32[]{:S(2)}) collective-permute-start(bf16[128,256]{1,0:T(8,128)(2,1)S(1)} %get-tuple-element.26), channel_id=1, source_target_pairs={{0,128},{8,136},{16,144},{24,152},{32,160},{40,168},{48,176},{56,1... | collective-permute-start | bytes 196616 | tf_op jit(solution)/shard_map/ppermute | solution.py:270
  138.6 7.7 %collective-permute-start.8 = (bf16[128,256]{1,0:T(8,128)(2,1)S(1)}, bf16[128,256]{1,0:T(8,128)(2,1)S(1)}, u32[]{:S(2)}, u32[]{:S(2)}) collective-permute-start(bf16[128,256]{1,0:T(8,128)(2,1)S(1)} %get-tuple-element.26), channel_id=1, source_target_pairs={{0,192},{8,200},{16,208},{24,216},{32,224},{40,232},{48,240},{56,2... | collective-permute-start | bytes 196616 | tf_op jit(solution)/shard_map/ppermute | solution.py:270
  140.5 7.2 %collective-permute-start.9 = (bf16[128,256]{1,0:T(8,128)(2,1)S(1)}, bf16[128,256]{1,0:T(8,128)(2,1)S(1)}, u32[]{:S(2)}, u32[]{:S(2)}) collective-permute-start(bf16[128,256]{1,0:T(8,128)(2,1)S(1)} %get-tuple-element.26), channel_id=1, source_target_pairs={{0,256},{8,264},{16,272},{24,280},{32,288},{40,296},{48,304},{56,3... | collective-permute-start | bytes 196616 | tf_op jit(solution)/shard_map/ppermute | solution.py:270
  141.8 9.5 %collective-permute-start.10 = (bf16[128,256]{1,0:T(8,128)(2,1)S(1)}, bf16[128,256]{1,0:T(8,128)(2,1)S(1)}, u32[]{:S(2)}, u32[]{:S(2)}) collective-permute-start(bf16[128,256]{1,0:T(8,128)(2,1)S(1)} %get-tuple-element.26), channel_id=1, source_target_pairs={{0,320},{8,328},{16,336},{24,344},{32,352},{40,360},{48,368},{56,3... | collective-permute-start | bytes 196616 | tf_op jit(solution)/shard_map/ppermute | solution.py:270
  143.2 10.1 %collective-permute-start.15 = (bf16[128,256]{1,0:T(8,128)(2,1)S(1)}, bf16[128,256]{1,0:T(8,128)(2,1)S(1)}, u32[]{:S(2)}, u32[]{:S(2)}) collective-permute-start(bf16[128,256]{1,0:T(8,128)(2,1)S(1)} %get-tuple-element.26), channel_id=1, source_target_pairs={{0,384},{8,392},{16,400},{24,408},{32,416},{40,424},{48,432},{56,4... | collective-permute-start | bytes 196616 | tf_op jit(solution)/shard_map/ppermute | solution.py:270
  151.4 14.8 %collective-permute-start.11 = (bf16[768,256]{1,0:T(8,128)(2,1)S(1)}, bf16[768,256]{1,0:T(8,128)(2,1)S(1)}, u32[]{:S(2)}, u32[]{:S(2)}) collective-permute-start(bf16[768,256]{1,0:T(8,128)(2,1)S(1)} %get-tuple-element.48), channel_id=1, source_target_pairs={{0,8},{8,16},{16,24},{24,32},{32,40},{40,48},{48,56},{56,64},{64,7... | collective-permute-start | bytes 1179656 | tf_op jit(solution)/shard_map/ppermute | solution.py:279
  153.3 14.7 %collective-permute-start.16 = (bf16[896,256]{1,0:T(8,128)(2,1)S(1)}, bf16[896,256]{1,0:T(8,128)(2,1)S(1)}, u32[]{:S(2)}, u32[]{:S(2)}) collective-permute-start(bf16[896,256]{1,0:T(8,128)(2,1)S(1)} %constant_dynamic-update-slice_fusion.8.refs_3_), channel_id=1, source_target_pairs={{0,56},{8,0},{16,8},{24,16},{32,24},{40,32},{48,40},{56,48},{1,57}... | collective-permute-start | bytes 1376264 | tf_op jit(solution)/shard_map/ppermute | solution.py:282
  166.2 13.9 %collective-permute-start.12 = (bf16[768,256]{1,0:T(8,128)(2,1)S(1)}, bf16[768,256]{1,0:T(8,128)(2,1)S(1)}, u32[]{:S(2)}, u32[]{:S(2)}) collective-permute-start(bf16[768,256]{1,0:T(8,128)(2,1)S(1)} %collective-permute-done.11.refs_3_), channel_id=1, source_target_pairs={{0,8},{8,16},{16,24},{24,32},{32,40},{40,48},{48,56},{56,64},{64,7... | collective-permute-start | bytes 1179656 | tf_op jit(solution)/shard_map/ppermute | solution.py:279
  168.1 14.0 %collective-permute-start.17 = (bf16[896,256]{1,0:T(8,128)(2,1)S(1)}, bf16[896,256]{1,0:T(8,128)(2,1)S(1)}, u32[]{:S(2)}, u32[]{:S(2)}) collective-permute-start(bf16[896,256]{1,0:T(8,128)(2,1)S(1)} %collective-permute-done.16.refs_4_), channel_id=1, source_target_pairs={{0,56},{8,0},{16,8},{24,16},{32,24},{40,32},{48,40},{56,48},{1,57}... | collective-permute-start | bytes 1376264 | tf_op jit(solution)/shard_map/ppermute | solution.py:282
  180.0 13.9 %collective-permute-start.13 = (bf16[768,256]{1,0:T(8,128)(2,1)S(1)}, bf16[768,256]{1,0:T(8,128)(2,1)S(1)}, u32[]{:S(2)}, u32[]{:S(2)}) collective-permute-start(bf16[768,256]{1,0:T(8,128)(2,1)S(1)} %collective-permute-done.12.refs_3_), channel_id=1, source_target_pairs={{0,8},{8,16},{16,24},{24,32},{32,40},{40,48},{48,56},{56,64},{64,7... | collective-permute-start | bytes 1179656 | tf_op jit(solution)/shard_map/ppermute | solution.py:279
  182.1 19.8 %collective-permute-start.18 = (bf16[896,256]{1,0:T(8,128)(2,1)S(1)}, bf16[896,256]{1,0:T(8,128)(2,1)S(1)}, u32[]{:S(2)}, u32[]{:S(2)}) collective-permute-start(bf16[896,256]{1,0:T(8,128)(2,1)S(1)} %collective-permute-done.17.refs_4_), channel_id=1, source_target_pairs={{0,56},{8,0},{16,8},{24,16},{32,24},{40,32},{48,40},{56,48},{1,57}... | collective-permute-start | bytes 1376264 | tf_op jit(solution)/shard_map/ppermute | solution.py:282
  184.2 0.9 copy-start.2
  193.9 14.6 %collective-permute-start.14 = (bf16[768,256]{1,0:T(8,128)(2,1)S(1)}, bf16[768,256]{1,0:T(8,128)(2,1)S(1)}, u32[]{:S(2)}, u32[]{:S(2)}) collective-permute-start(bf16[768,256]{1,0:T(8,128)(2,1)S(1)} %collective-permute-done.13.refs_3_), channel_id=1, source_target_pairs={{0,8},{8,16},{16,24},{24,32},{32,40},{40,48},{48,56},{56,64},{64,7... | collective-permute-start | bytes 1179656 | tf_op jit(solution)/shard_map/ppermute | solution.py:279
